TPU v7x, 32 devices: a whole 2x2x4 slice. The times are simulated.
32 devices in a mesh: row: 4 (over y, core), col: 8 (over z, x).
Axes of the slice: x: 2, y: 2, z: 4, core: 2. Of those that a mesh axis runs over, the one named last changes fastest.
Arguments:
- transmission: float32 [2, 2, 2048, 2048], P(None, None, 'row', 'col'), may hold values from -5 to 5
- probe_field: float32 [2, 256, 256], replicated, may hold values from -6 to 6
- prop_phase: float32 [256, 256], replicated, may hold values from -3.140625 to 3.140625
- amplitude: float32 [4, 8, 4, 256, 256], P('row', 'col'), may hold values from 0 to 2
- window_count: int32 [4, 8], P('row', 'col'), may hold values from 1 to 4
- offset_row: int32 [4, 8, 4], P('row', 'col'), may hold values from 0 to 384
- offset_col: int32 [4, 8, 4], P('row', 'col'), may hold values from 0 to 128
- window_batch: int32 [4, 8, 4], P('row', 'col'), may hold values from 0 to 2
Outputs:
- updated: float32 [2, 2, 2048, 2048], P(None, None, 'row', 'col')
All inputs are finite; a program needn't handle non-finite values.
Results may differ from a plain program's by a relative error of at most 0.0003.
Values sent between devices are 32-bit elements; how exact they have to be, the bound alone decides.
A program may use at most 64 MiB of HBM per device.

v0:
```python
import functools
import math

import jax
import jax.numpy as jnp
import numpy as np
import ml_dtypes
from jax import lax
from jax.experimental import pallas as pl
from jax.experimental.pallas import tpu as pltpu
from jax.sharding import PartitionSpec as P

BATCHES = 3
STEP = 0.5
VMEM_LIMIT = 50 * 1024 * 1024


def shifted(array, axis, by):
    size = lax.axis_size(axis)
    pairs = [(i, i + by) for i in range(size) if 0 <= i + by < size]
    return lax.ppermute(array, axis, pairs)


def tables(length):
    index = np.arange(length)
    angle = (index[:, None] * index[None, :] % length) * (-2.0 * math.pi / length)
    scale = 1.0 / math.sqrt(length)
    re, im = np.cos(angle) * scale, np.sin(angle) * scale
    right = np.block([[re, im], [-im, re]]).astype(np.float32)
    high = right.astype(ml_dtypes.bfloat16)
    low = (right - high.astype(np.float32)).astype(ml_dtypes.bfloat16)
    stacked = np.concatenate([high, high, low], axis=0)
    return stacked, np.ascontiguousarray(stacked.T)


def split(value):
    high = value.astype(jnp.bfloat16)
    low = (value - high.astype(jnp.float32)).astype(jnp.bfloat16)
    return high, low


def forward(re, im, right_ref, left_ref):
    n = re.shape[0]
    (rh, rl), (ih, il) = split(re), split(im)
    y = jnp.dot(
        jnp.concatenate([rh, ih, rl, il, rh, ih], axis=1),
        right_ref[...],
        preferred_element_type=jnp.float32,
    )
    (rh, rl), (ih, il) = split(y[:, :n]), split(y[:, n:])
    z = jnp.dot(
        left_ref[...],
        jnp.concatenate([rh, ih, rl, il, rh, ih], axis=0),
        preferred_element_type=jnp.float32,
    )
    return z[:n], z[n:]


def inverse(re, im, right_ref, left_ref):
    out_im, out_re = forward(im, re, right_ref, left_ref)
    return out_re, out_im


def window_kernel(batch, first, last, *refs):
    count, row_off, col_off, which, keep = refs[:5]
    n_in = 4 if first else 8
    pieces = refs[5 : 5 + n_in]
    rest = refs[5 + n_in :]
    probe, prop, amplitude, right_t, left_t = rest[:5]
    rest = rest[5:]
    if last:
        base, down, right_one, right_two, ext, delta = rest
    else:
        base, down, up, right_one, left_one, ext, delta = rest
    win = probe.shape[1]
    strip = win // 2
    rows = ext.shape[2] - 8 - strip
    cols = ext.shape[3] - strip
    wide = cols + strip
    slots = amplitude.shape[0]

    if first:
        current, below, side, corner = pieces
        for a in range(2):
            for b in range(2):
                ext[a, b, :rows, :cols] = current[a, b]
                ext[a, b, rows : rows + strip, :cols] = below[a, b]
                ext[a, b, :rows, cols:] = side[a, b]
                ext[a, b, rows : rows + strip, cols:] = corner[a, b]
    else:
        old, from_up, from_down, fr_one, fr_two, fl_one, fl_two, corner = pieces
        keep_row = keep[0].astype(jnp.float32)
        keep_col = keep[1].astype(jnp.float32)
        for a in range(2):
            for b in range(2):
                ext[a, b, :strip, :strip] = old[a, b, :strip, :strip] + from_up[a, b, :, :strip] + fr_two[a, b]
                ext[a, b, :strip, strip:cols] = old[a, b, :strip, strip:cols] + from_up[a, b, :, strip:cols]
                ext[a, b, :strip, cols:] = (
                    old[a, b, :strip, cols:] + from_up[a, b, :, cols:] + fl_two[a, b]
                ) * keep_col
                ext[a, b, strip:rows, :strip] = old[a, b, strip:rows, :strip] + fr_one[a, b]
                ext[a, b, strip:rows, strip:cols] = old[a, b, strip:rows, strip:cols]
                ext[a, b, strip:rows, cols:] = (old[a, b, strip:rows, cols:] + fl_one[a, b]) * keep_col
                bottom = pl.ds(rows, strip)
                ext[a, b, bottom, :strip] = (
                    old[a, b, bottom, :strip] + from_down[a, b, :, :strip] + corner[a, b, :, :strip]
                ) * keep_row
                ext[a, b, bottom, strip:cols] = (
                    old[a, b, bottom, strip:cols] + from_down[a, b, :, strip:cols]
                ) * keep_row
                ext[a, b, bottom, cols:] = (
                    old[a, b, bottom, cols:] + from_down[a, b, :, cols:] + corner[a, b, :, strip:]
                ) * (keep_row * keep_col)
    for a in range(2):
        for b in range(2):
            delta[a, b] = jnp.zeros(delta.shape[2:], jnp.float32)

    def visit(slot, carry):
        @pl.when((slot < count[0, 0]) & (which[0, 0, slot] == batch))
        def _():
            top = row_off[0, 0, slot]
            shift_c = col_off[0, 0, slot]
            origin = pl.multiple_of((top // 8) * 8, 8)
            shift_r = top - origin
            tail = pl.multiple_of(origin + win, 8)
            in_tail = lax.broadcasted_iota(jnp.int32, (8, wide), 0) < shift_r
            in_side = lax.broadcasted_iota(jnp.int32, (win, strip), 1) < shift_c

            def window(a, b):
                head = jnp.where(in_tail, ext[a, b, pl.ds(tail, 8), :], ext[a, b, pl.ds(origin, 8), :])
                body = ext[a, b, pl.ds(origin + 8, win - 8), :]
                full = jnp.concatenate([head, body], axis=0)
                near = jnp.where(in_side, full[:, cols:], full[:, :strip])
                return jnp.concatenate([near, full[:, strip:cols]], axis=1)

            def add(a, b, value):
                value = value * (-STEP)
                near = value[:, :strip]
                zero = jnp.zeros_like(near)
                full = jnp.concatenate(
                    [jnp.where(in_side, zero, near), value[:, strip:], jnp.where(in_side, near, zero)], axis=1
                )
                head = full[:8]
                nothing = jnp.zeros_like(head)
                delta[a, b, pl.ds(origin, 8), :] += jnp.where(in_tail, nothing, head)
                delta[a, b, pl.ds(origin + 8, win - 8), :] += full[8:]
                delta[a, b, pl.ds(tail, 8), :] += jnp.where(in_tail, head, nothing)

            pr = pltpu.roll(pltpu.roll(probe[0], shift_c, 1), shift_r, 0)
            pi = pltpu.roll(pltpu.roll(probe[1], shift_c, 1), shift_r, 0)
            wr, wi = window(0, 0), window(0, 1)
            fr, fi = forward(pr * wr - pi * wi, pr * wi + pi * wr, right_t, left_t)
            hr, hi = prop[0], prop[1]
            br, bi = inverse(hr * fr - hi * fi, hr * fi + hi * fr, right_t, left_t)
            wr, wi = window(1, 0), window(1, 1)
            fr, fi = forward(br * wr - bi * wi, br * wi + bi * wr, right_t, left_t)
            factor = 1.0 - amplitude[slot] * lax.rsqrt(jnp.maximum(fr * fr + fi * fi, 1.0))
            gr, gi = inverse(fr * factor, fi * factor, right_t, left_t)
            add(1, 0, br * gr + bi * gi)
            add(1, 1, br * gi - bi * gr)
            fr, fi = forward(wr * gr + wi * gi, wr * gi - wi * gr, right_t, left_t)
            hr, hi = prop[0], prop[1]
            gr, gi = inverse(hr * fr + hi * fi, hr * fi - hi * fr, right_t, left_t)
            add(0, 0, pr * gr + pi * gi)
            add(0, 1, pr * gi - pi * gr)

        return carry

    lax.fori_loop(0, slots, visit, 0)
    for a in range(2):
        for b in range(2):
            if last:
                base[a, b] = ext[a, b, :rows, :cols] + delta[a, b, :rows, :cols]
                right_two[a, b] = delta[a, b, :strip, cols:]
            else:
                base[a, b] = ext[a, b, : rows + strip] + delta[a, b, : rows + strip]
                up[a, b] = delta[a, b, :strip]
                left_one[a, b] = delta[a, b, strip:rows, :strip]
            down[a, b] = delta[a, b, rows : rows + strip]
            right_one[a, b] = delta[a, b, strip:rows, cols:]


def finish_kernel(base, from_up, fr_one, fr_two, out):
    rows, cols = out.shape[2:]
    strip = from_up.shape[2]
    for a in range(2):
        for b in range(2):
            out[a, b, :strip, :strip] = base[a, b, :strip, :strip] + from_up[a, b, :, :strip] + fr_two[a, b]
            out[a, b, :strip, strip:] = base[a, b, :strip, strip:] + from_up[a, b, :, strip:cols]
            out[a, b, strip:, :strip] = base[a, b, strip:, :strip] + fr_one[a, b]
            out[a, b, strip:, strip:] = base[a, b, strip:, strip:]


def body(
    transmission, probe, prop_phase, amplitude, window_count, offset_row, offset_col, window_batch
):
    win = probe.shape[1]
    strip = win // 2
    rows, cols = transmission.shape[2:]
    wide = cols + strip
    right_t, left_t = (jnp.asarray(t) for t in tables(win))
    prop = jnp.stack([jnp.cos(prop_phase), jnp.sin(prop_phase)])
    measured = amplitude[0, 0]
    keep = jnp.stack(
        [
            (lax.axis_index("row") < lax.axis_size("row") - 1).astype(jnp.int32),
            (lax.axis_index("col") < lax.axis_size("col") - 1).astype(jnp.int32),
        ]
    )
    smem = pl.BlockSpec(memory_space=pltpu.SMEM)
    vmem = pl.BlockSpec(memory_space=pltpu.VMEM)

    def shape(r, c):
        return jax.ShapeDtypeStruct((2, 2, r, c), jnp.float32)

    def windows(batch, pieces):
        first, last = batch == 0, batch == BATCHES - 1
        if last:
            outs = (shape(rows, cols), shape(strip, wide), shape(rows - strip, strip), shape(strip, strip))
        else:
            outs = (
                shape(rows + strip, wide),
                shape(strip, wide),
                shape(strip, wide),
                shape(rows - strip, strip),
                shape(rows - strip, strip),
            )
        return pl.pallas_call(
            functools.partial(window_kernel, batch, first, last),
            out_shape=outs,
            in_specs=[smem] * 5 + [vmem] * (len(pieces) + 5),
            out_specs=[vmem] * len(outs),
            scratch_shapes=[
                pltpu.VMEM((2, 2, rows + strip + 8, wide), jnp.float32),
                pltpu.VMEM((2, 2, rows + strip + 8, wide), jnp.float32),
            ],
            compiler_params=pltpu.CompilerParams(vmem_limit_bytes=VMEM_LIMIT),
            name=f"windows{batch}",
        )(
            window_count, offset_row, offset_col, window_batch, keep, *pieces,
            probe, prop, measured, right_t, left_t,
        )

    side = shifted(transmission[:, :, :, :strip], "col", -1)
    below = shifted(transmission[:, :, :strip, :], "row", -1)
    corner = shifted(side[:, :, :strip, :], "row", -1)
    pieces = (transmission, below, side, corner)
    for batch in range(BATCHES - 1):
        base, down, up, right_one, left_one = windows(batch, pieces)
        from_up = shifted(down, "row", 1)
        from_down = shifted(up, "row", -1)
        fr_one = shifted(right_one, "col", 1)
        fl_one = shifted(left_one, "col", -1)
        fr_two = shifted(up[..., cols:] + from_up[..., cols:], "col", 1)
        fl_two = shifted(up[..., :strip] + from_up[..., :strip], "col", -1)
        corner = shifted(jnp.concatenate([fr_two, fl_two], axis=3), "row", -1)
        pieces = (base, from_up, from_down, fr_one, fr_two, fl_one, fl_two, corner)
    base, down, right_one, right_two = windows(BATCHES - 1, pieces)
    from_up = shifted(down, "row", 1)
    fr_one = shifted(right_one, "col", 1)
    fr_two = shifted(right_two + from_up[..., cols:], "col", 1)
    return pl.pallas_call(
        finish_kernel,
        out_shape=shape(rows, cols),
        in_specs=[vmem] * 4,
        out_specs=vmem,
        compiler_params=pltpu.CompilerParams(vmem_limit_bytes=VMEM_LIMIT),
        name="finish",
    )(base, from_up, fr_one, fr_two)


def solution(mesh):
    in_specs = (
        P(None, None, "row", "col"),
        P(),
        P(),
        P("row", "col", None, None, None),
        P("row", "col"),
        P("row", "col", None),
        P("row", "col", None),
        P("row", "col", None),
    )
    out_specs = P(None, None, "row", "col")
    return jax.shard_map(body, mesh=mesh, in_specs=in_specs, out_specs=out_specs, check_vma=False)
```

profile of v0, /device:TPU:16, one launch (start us, length us, event | category | flops | bytes accessed | tf_op | source)
XLA Modules:
  0.0 267.2 jit_solution(8584278066426696496)
XLA Ops:
  0.0 1.3 slice.37
  1.4 3.4 %collective-permute-start.1 = (f32[2,2,512,128]{3,2,1,0:T(8,128)S(1)}, f32[2,2,512,128]{3,2,1,0:T(8,128)S(1)}, u32[]{:S(2)}, u32[]{:S(2)}) collective-permute-start(f32[2,2,512,128]{3,2,1,0:T(8,128)S(1)} %slice.37), channel_id=1, source_target_pairs={{1,0},{2,1},{3,2},{4,3},{5,4},{6,5},{7,6},{9,8},{10,9},{11,10},{12... | collective-permute-start | bytes 3145736 | tf_op jit(solution)/shard_map/ppermute | solution.py:21
  5.9 1.3 collective-permute-start
  7.2 21.1 %collective-permute-done.1.refs_7_ = f32[2,2,512,128]{3,2,1,0:T(8,128)S(1)} collective-permute-done((f32[2,2,512,128]{3,2,1,0:T(8,128)S(1)}, f32[2,2,512,128]{3,2,1,0:T(8,128)S(1)}, u32[]{:S(2)}, u32[]{:S(2)}) %collective-permute-start.1) | collective-permute-done | bytes 1048608 | tf_op jit(solution)/shard_map/ppermute | solution.py:21
  32.8 16.3 %windows0.1 = (f32[2,2,640,384]{3,2,1,0:T(8,128)}, f32[2,2,128,384]{3,2,1,0:T(8,128)S(1)}, f32[2,2,128,384]{3,2,1,0:T(8,128)S(1)}, f32[2,2,384,128]{3,2,1,0:T(8,128)}, f32[2,2,384,128]{3,2,1,0:T(8,128)}) custom-call(s32[1,1]{1,0:T(1,128)S(6)} %copy.11.refs_0_, s32[1,1,4]{2,1,0:T(1,128)S(1)} %copy-done.2, s32[1,1,4]{2,1,0:T(1,128)S(1)} %copy-done.3, ...), custom_call_target="tpu_custom_call" | custom-call | tf_op jit(solution)/shard_map/windows0/pallas_call | solution.py:228
  49.0 6.2 %collective-permute-start.3 = (f32[2,2,128,384]{3,2,1,0:T(8,128)S(1)}, f32[2,2,128,384]{3,2,1,0:T(8,128)S(1)}, u32[]{:S(2)}, u32[]{:S(2)}) collective-permute-start(f32[2,2,128,384]{3,2,1,0:T(8,128)S(1)} %get-tuple-element.20), channel_id=1, source_target_pairs={{0,8},{8,16},{16,24},{1,9},{9,17},{17,25},{2,10},{10,18},{18,26},{... | collective-permute-start | bytes 2359304 | tf_op jit(solution)/shard_map/ppermute | solution.py:21
  55.3 1.8 collective-permute-done.3.refs_6_
  57.2 1.9 collective-permute-start.8
  59.1 29.4 %collective-permute-start.6 = (f32[2,2,128,128]{3,2,1,0:T(8,128)S(1)}, f32[2,2,128,128]{3,2,1,0:T(8,128)S(1)}, u32[]{:S(2)}, u32[]{:S(2)}) collective-permute-start(f32[2,2,128,128]{3,2,1,0:T(8,128)S(1)} %get-tuple-element.36), channel_id=1, source_target_pairs={{0,1},{1,2},{2,3},{3,4},{4,5},{5,6},{6,7},{8,9},{9,10},{10,11},{11... | collective-permute-start | bytes 786440 | tf_op jit(solution)/shard_map/ppermute | solution.py:21
  88.5 4.8 %collective-permute-start.5 = (f32[2,2,384,128]{3,2,1,0:T(8,128)}, f32[2,2,384,128]{3,2,1,0:T(8,128)S(1)}, u32[]{:S(2)}, u32[]{:S(2)}) collective-permute-start(f32[2,2,384,128]{3,2,1,0:T(8,128)} %get-tuple-element.22), channel_id=1, source_target_pairs={{0,1},{1,2},{2,3},{3,4},{4,5},{5,6},{6,7},{8,9},{9,10},{10,11},{11... | collective-permute-start | bytes 2359304 | tf_op jit(solution)/shard_map/ppermute | solution.py:21
  93.3 1.9 collective-permute-start.7
  95.2 1.3 collective-permute-start.4
  96.5 19.5 %collective-permute-done.6.refs_9_ = f32[2,2,128,128]{3,2,1,0:T(8,128)S(1)} collective-permute-done((f32[2,2,128,128]{3,2,1,0:T(8,128)S(1)}, f32[2,2,128,128]{3,2,1,0:T(8,128)S(1)}, u32[]{:S(2)}, u32[]{:S(2)}) %collective-permute-start.6) | collective-permute-done | bytes 262176 | tf_op jit(solution)/shard_map/ppermute | solution.py:21
  116.1 1.5 collective-permute-start.9
  117.5 15.4 %collective-permute-done.5.refs_8_ = f32[2,2,384,128]{3,2,1,0:T(8,128)S(1)} collective-permute-done((f32[2,2,384,128]{3,2,1,0:T(8,128)}, f32[2,2,384,128]{3,2,1,0:T(8,128)S(1)}, u32[]{:S(2)}, u32[]{:S(2)}) %collective-permute-start.5) | collective-permute-done | bytes 786464 | tf_op jit(solution)/shard_map/ppermute | solution.py:21
  134.3 7.6 %windows1.1 = (f32[2,2,640,384]{3,2,1,0:T(8,128)}, f32[2,2,128,384]{3,2,1,0:T(8,128)S(1)}, f32[2,2,128,384]{3,2,1,0:T(8,128)S(1)}, f32[2,2,384,128]{3,2,1,0:T(8,128)}, f32[2,2,384,128]{3,2,1,0:T(8,128)}) custom-call(s32[1,1]{1,0:T(1,128)S(6)} %copy.11.refs_0_, s32[1,1,4]{2,1,0:T(1,128)S(1)} %copy-done.2, s32[1,1,4]{2,1,0:T(1,128)S(1)} %copy-done.3, ...), custom_call_target="tpu_custom_call" | custom-call | tf_op jit(solution)/shard_map/windows1/pallas_call | solution.py:228
  142.0 2.0 collective-permute-start.10
  144.0 1.8 collective-permute-done.10.refs_6_
  145.9 3.0 %collective-permute-start.15 = (f32[2,2,128,128]{3,2,1,0:T(8,128)S(1)}, f32[2,2,128,128]{3,2,1,0:T(8,128)S(1)}, u32[]{:S(2)}, u32[]{:S(2)}) collective-permute-start(f32[2,2,128,128]{3,2,1,0:T(8,128)S(1)} %get-tuple-element.33), channel_id=1, source_target_pairs={{1,0},{2,1},{3,2},{4,3},{5,4},{6,5},{7,6},{9,8},{10,9},{11,10},{12... | collective-permute-start | bytes 786440 | tf_op jit(solution)/shard_map/ppermute | solution.py:21
  148.9 13.2 %collective-permute-start.13 = (f32[2,2,128,128]{3,2,1,0:T(8,128)S(1)}, f32[2,2,128,128]{3,2,1,0:T(8,128)S(1)}, u32[]{:S(2)}, u32[]{:S(2)}) collective-permute-start(f32[2,2,128,128]{3,2,1,0:T(8,128)S(1)} %get-tuple-element.34), channel_id=1, source_target_pairs={{0,1},{1,2},{2,3},{3,4},{4,5},{5,6},{6,7},{8,9},{9,10},{10,11},{11... | collective-permute-start | bytes 786440 | tf_op jit(solution)/shard_map/ppermute | solution.py:21
  162.1 4.8 %collective-permute-start.12 = (f32[2,2,384,128]{3,2,1,0:T(8,128)}, f32[2,2,384,128]{3,2,1,0:T(8,128)S(1)}, u32[]{:S(2)}, u32[]{:S(2)}) collective-permute-start(f32[2,2,384,128]{3,2,1,0:T(8,128)} %get-tuple-element.27), channel_id=1, source_target_pairs={{0,1},{1,2},{2,3},{3,4},{4,5},{5,6},{6,7},{8,9},{9,10},{10,11},{11... | collective-permute-start | bytes 2359304 | tf_op jit(solution)/shard_map/ppermute | solution.py:21
  166.9 1.9 collective-permute-start.14
  170.2 1.5 collective-permute-start.16
  171.7 33.0 %collective-permute-done.12.refs_8_ = f32[2,2,384,128]{3,2,1,0:T(8,128)S(1)} collective-permute-done((f32[2,2,384,128]{3,2,1,0:T(8,128)}, f32[2,2,384,128]{3,2,1,0:T(8,128)S(1)}, u32[]{:S(2)}, u32[]{:S(2)}) %collective-permute-start.12) | collective-permute-done | bytes 786464 | tf_op jit(solution)/shard_map/ppermute | solution.py:21
  206.2 6.5 %windows2.1 = (f32[2,2,512,256]{3,2,1,0:T(8,128)}, f32[2,2,128,384]{3,2,1,0:T(8,128)S(1)}, f32[2,2,384,128]{3,2,1,0:T(8,128)S(1)}, f32[2,2,128,128]{3,2,1,0:T(8,128)S(1)}) custom-call(s32[1,1]{1,0:T(1,128)S(6)} %copy.11.refs_0_, s32[1,1,4]{2,1,0:T(1,128)S(1)} %copy-done.2, s32[1,1,4]{2,1,0:T(1,128)S(1)} %copy-done.3, s32[1,1,4]{2,1,0:T(1,128)S(1)} %copy-done.4, ...), custom_call_target="tpu_custom_call" | custom-call | tf_op jit(solution)/shard_map/windows2/pallas_call | solution.py:228
  212.7 14.9 %collective-permute-start.17 = (f32[2,2,128,384]{3,2,1,0:T(8,128)S(1)}, f32[2,2,128,384]{3,2,1,0:T(8,128)S(1)}, u32[]{:S(2)}, u32[]{:S(2)}) collective-permute-start(f32[2,2,128,384]{3,2,1,0:T(8,128)S(1)} %get-tuple-element.30), channel_id=1, source_target_pairs={{0,8},{8,16},{16,24},{1,9},{9,17},{17,25},{2,10},{10,18},{18,26},{... | collective-permute-start | bytes 2359304 | tf_op jit(solution)/shard_map/ppermute | solution.py:21
  227.6 13.9 %collective-permute-start.18 = (f32[2,2,384,128]{3,2,1,0:T(8,128)S(1)}, f32[2,2,384,128]{3,2,1,0:T(8,128)S(1)}, u32[]{:S(2)}, u32[]{:S(2)}) collective-permute-start(f32[2,2,384,128]{3,2,1,0:T(8,128)S(1)} %get-tuple-element.31), channel_id=1, source_target_pairs={{0,1},{1,2},{2,3},{3,4},{4,5},{5,6},{6,7},{8,9},{9,10},{10,11},{11... | collective-permute-start | bytes 2359304 | tf_op jit(solution)/shard_map/ppermute | solution.py:21
  241.6 1.9 collective-permute-start.19
  243.5 15.9 %collective-permute-done.18.fr_one = f32[2,2,384,128]{3,2,1,0:T(8,128)S(1)} collective-permute-done((f32[2,2,384,128]{3,2,1,0:T(8,128)S(1)}, f32[2,2,384,128]{3,2,1,0:T(8,128)S(1)}, u32[]{:S(2)}, u32[]{:S(2)}) %collective-permute-start.18) | collective-permute-done | bytes 786464 | tf_op jit(solution)/shard_map/ppermute | solution.py:21
  259.5 4.6 %collective-permute-done.19.fr_two = f32[2,2,128,128]{3,2,1,0:T(8,128)S(1)} collective-permute-done((f32[2,2,128,128]{3,2,1,0:T(8,128)S(1)}, f32[2,2,128,128]{3,2,1,0:T(8,128)S(1)}, u32[]{:S(2)}, u32[]{:S(2)}) %collective-permute-start.19) | collective-permute-done | bytes 262176 | tf_op jit(solution)/shard_map/ppermute | solution.py:21
  264.1 1.6 copy-done.1
  265.7 1.5 finish.1
  (53 shorter events, 9.2 us)
Async XLA Ops:
  0.0 30.4 %copy-start.14 = (f32[256,256]{1,0:T(8,128)S(1)}, f32[256,256]{1,0:T(8,128)}, u32[]{:S(2)}) copy-start(f32[256,256]{1,0:T(8,128)} %param.12) | copy-start | bytes 786436
  1.3 31.4 %copy-start = (f32[2,256,256]{2,1,0:T(8,128)S(1)}, f32[2,256,256]{2,1,0:T(8,128)}, u32[]{:S(2)}) copy-start(f32[2,256,256]{2,1,0:T(8,128)} %refs_13_.4) | copy-start | bytes 1572868
  1.4 31.4 %copy-start.2 = (s32[1,1,4]{2,1,0:T(1,128)S(1)}, s32[1,1,4]{2,1,0:T(1,128)}, u32[]{:S(2)}) copy-start(s32[1,1,4]{2,1,0:T(1,128)} %refs_1_.5) | copy-start | bytes 52
  1.4 31.4 %copy-start.3 = (s32[1,1,4]{2,1,0:T(1,128)S(1)}, s32[1,1,4]{2,1,0:T(1,128)}, u32[]{:S(2)}) copy-start(s32[1,1,4]{2,1,0:T(1,128)} %refs_2_.5) | copy-start | bytes 52
  1.4 31.4 %copy-start.4 = (s32[1,1,4]{2,1,0:T(1,128)S(1)}, s32[1,1,4]{2,1,0:T(1,128)}, u32[]{:S(2)}) copy-start(s32[1,1,4]{2,1,0:T(1,128)} %refs_3_.5) | copy-start | bytes 52
  1.4 26.9 %collective-permute-start.1 = (f32[2,2,512,128]{3,2,1,0:T(8,128)S(1)}, f32[2,2,512,128]{3,2,1,0:T(8,128)S(1)}, u32[]{:S(2)}, u32[]{:S(2)}) collective-permute-start(f32[2,2,512,128]{3,2,1,0:T(8,128)S(1)} %slice.37), channel_id=1, source_target_pairs={{1,0},{2,1},{3,2},{4,3},{5,4},{6,5},{7,6},{9,8},{10,9},{11,10},{12... | collective-permute-start | bytes 3145736 | tf_op jit(solution)/shard_map/ppermute | solution.py:21
  5.9 26.3 %collective-permute-start = (f32[2,2,128,256]{3,2,1,0:T(8,128)S(1)}, f32[2,2,128,256]{3,2,1,0:T(8,128)S(1)}, u32[]{:S(2)}, u32[]{:S(2)}) collective-permute-start(f32[2,2,128,256]{3,2,1,0:T(8,128)S(1)} %slice.36), channel_id=1, source_target_pairs={{8,0},{16,8},{24,16},{9,1},{17,9},{25,17},{10,2},{18,10},{26,18},{... | collective-permute-start | bytes 1572872 | tf_op jit(solution)/shard_map/ppermute | solution.py:21
  28.3 4.4 %copy-start.7 = (f32[2,2,512,128]{3,2,1,0:T(8,128)}, f32[2,2,512,128]{3,2,1,0:T(8,128)S(1)}, u32[]{:S(2)}) copy-start(f32[2,2,512,128]{3,2,1,0:T(8,128)S(1)} %collective-permute-done.1.refs_7_) | copy-start | bytes 3145732
  29.1 3.6 %collective-permute-start.2 = (f32[2,2,128,128]{3,2,1,0:T(8,128)}, f32[2,2,128,128]{3,2,1,0:T(8,128)S(1)}, u32[]{:S(2)}, u32[]{:S(2)}) collective-permute-start(f32[2,2,128,128]{3,2,1,0:T(8,128)} %slice.48), channel_id=1, source_target_pairs={{8,0},{16,8},{24,16},{9,1},{17,9},{25,17},{10,2},{18,10},{26,18},{... | collective-permute-start | bytes 786440 | tf_op jit(solution)/shard_map/ppermute | solution.py:21
  49.0 8.1 %collective-permute-start.3 = (f32[2,2,128,384]{3,2,1,0:T(8,128)S(1)}, f32[2,2,128,384]{3,2,1,0:T(8,128)S(1)}, u32[]{:S(2)}, u32[]{:S(2)}) collective-permute-start(f32[2,2,128,384]{3,2,1,0:T(8,128)S(1)} %get-tuple-element.20), channel_id=1, source_target_pairs={{0,8},{8,16},{16,24},{1,9},{9,17},{17,25},{2,10},{10,18},{18,26},{... | collective-permute-start | bytes 2359304 | tf_op jit(solution)/shard_map/ppermute | solution.py:21
  57.1 75.9 %copy-start.6 = (f32[2,2,128,384]{3,2,1,0:T(8,128)}, f32[2,2,128,384]{3,2,1,0:T(8,128)S(1)}, u32[]{:S(2)}) copy-start(f32[2,2,128,384]{3,2,1,0:T(8,128)S(1)} %collective-permute-done.3.refs_6_) | copy-start | bytes 2359300
  57.2 39.4 %collective-permute-start.8 = (f32[2,2,128,128]{3,2,1,0:T(8,128)S(1)}, f32[2,2,128,128]{3,2,1,0:T(8,128)S(1)}, u32[]{:S(2)}, u32[]{:S(2)}) collective-permute-start(f32[2,2,128,128]{3,2,1,0:T(8,128)S(1)} %get-tuple-element.35), channel_id=1, source_target_pairs={{1,0},{2,1},{3,2},{4,3},{5,4},{6,5},{7,6},{9,8},{10,9},{11,10},{12... | collective-permute-start | bytes 786440 | tf_op jit(solution)/shard_map/ppermute | solution.py:21
  59.1 56.9 %collective-permute-start.6 = (f32[2,2,128,128]{3,2,1,0:T(8,128)S(1)}, f32[2,2,128,128]{3,2,1,0:T(8,128)S(1)}, u32[]{:S(2)}, u32[]{:S(2)}) collective-permute-start(f32[2,2,128,128]{3,2,1,0:T(8,128)S(1)} %get-tuple-element.36), channel_id=1, source_target_pairs={{0,1},{1,2},{2,3},{3,4},{4,5},{5,6},{6,7},{8,9},{9,10},{10,11},{11... | collective-permute-start | bytes 786440 | tf_op jit(solution)/shard_map/ppermute | solution.py:21
  88.5 44.5 %collective-permute-start.5 = (f32[2,2,384,128]{3,2,1,0:T(8,128)}, f32[2,2,384,128]{3,2,1,0:T(8,128)S(1)}, u32[]{:S(2)}, u32[]{:S(2)}) collective-permute-start(f32[2,2,384,128]{3,2,1,0:T(8,128)} %get-tuple-element.22), channel_id=1, source_target_pairs={{0,1},{1,2},{2,3},{3,4},{4,5},{5,6},{6,7},{8,9},{9,10},{10,11},{11... | collective-permute-start | bytes 2359304 | tf_op jit(solution)/shard_map/ppermute | solution.py:21
  93.3 39.6 %collective-permute-start.7 = (f32[2,2,384,128]{3,2,1,0:T(8,128)}, f32[2,2,384,128]{3,2,1,0:T(8,128)S(1)}, u32[]{:S(2)}, u32[]{:S(2)}) collective-permute-start(f32[2,2,384,128]{3,2,1,0:T(8,128)} %get-tuple-element.23), channel_id=1, source_target_pairs={{1,0},{2,1},{3,2},{4,3},{5,4},{6,5},{7,6},{9,8},{10,9},{11,10},{12... | collective-permute-start | bytes 2359304 | tf_op jit(solution)/shard_map/ppermute | solution.py:21
  95.2 37.7 %collective-permute-start.4 = (f32[2,2,128,384]{3,2,1,0:T(8,128)S(1)}, f32[2,2,128,384]{3,2,1,0:T(8,128)S(1)}, u32[]{:S(2)}, u32[]{:S(2)}) collective-permute-start(f32[2,2,128,384]{3,2,1,0:T(8,128)S(1)} %get-tuple-element.21), channel_id=1, source_target_pairs={{8,0},{16,8},{24,16},{9,1},{17,9},{25,17},{10,2},{18,10},{26,18},{... | collective-permute-start | bytes 2359304 | tf_op jit(solution)/shard_map/ppermute | solution.py:21
  116.1 16.9 %collective-permute-start.9 = (f32[2,2,128,256]{3,2,1,0:T(8,128)S(1)}, f32[2,2,128,256]{3,2,1,0:T(8,128)S(1)}, u32[]{:S(2)}, u32[]{:S(2)}) collective-permute-start(f32[2,2,128,256]{3,2,1,0:T(8,128)S(1)} %pad_maximum_fusion.1), channel_id=1, source_target_pairs={{8,0},{16,8},{24,16},{9,1},{17,9},{25,17},{10,2},{18,10},{26,18},{... | collective-permute-start | bytes 1572872 | tf_op jit(solution)/shard_map/ppermute | solution.py:21
  132.9 1.2 copy-start.12
  132.9 1.4 copy-start.13
  142.0 3.9 %collective-permute-start.10 = (f32[2,2,128,384]{3,2,1,0:T(8,128)S(1)}, f32[2,2,128,384]{3,2,1,0:T(8,128)S(1)}, u32[]{:S(2)}, u32[]{:S(2)}) collective-permute-start(f32[2,2,128,384]{3,2,1,0:T(8,128)S(1)} %get-tuple-element.25), channel_id=1, source_target_pairs={{0,8},{8,16},{16,24},{1,9},{9,17},{17,25},{2,10},{10,18},{18,26},{... | collective-permute-start | bytes 2359304 | tf_op jit(solution)/shard_map/ppermute | solution.py:21
  145.8 58.9 %copy-start.5 = (f32[2,2,128,384]{3,2,1,0:T(8,128)}, f32[2,2,128,384]{3,2,1,0:T(8,128)S(1)}, u32[]{:S(2)}) copy-start(f32[2,2,128,384]{3,2,1,0:T(8,128)S(1)} %collective-permute-done.10.refs_6_) | copy-start | bytes 2359300
  145.9 24.3 %collective-permute-start.15 = (f32[2,2,128,128]{3,2,1,0:T(8,128)S(1)}, f32[2,2,128,128]{3,2,1,0:T(8,128)S(1)}, u32[]{:S(2)}, u32[]{:S(2)}) collective-permute-start(f32[2,2,128,128]{3,2,1,0:T(8,128)S(1)} %get-tuple-element.33), channel_id=1, source_target_pairs={{1,0},{2,1},{3,2},{4,3},{5,4},{6,5},{7,6},{9,8},{10,9},{11,10},{12... | collective-permute-start | bytes 786440 | tf_op jit(solution)/shard_map/ppermute | solution.py:21
  148.9 21.3 %collective-permute-start.13 = (f32[2,2,128,128]{3,2,1,0:T(8,128)S(1)}, f32[2,2,128,128]{3,2,1,0:T(8,128)S(1)}, u32[]{:S(2)}, u32[]{:S(2)}) collective-permute-start(f32[2,2,128,128]{3,2,1,0:T(8,128)S(1)} %get-tuple-element.34), channel_id=1, source_target_pairs={{0,1},{1,2},{2,3},{3,4},{4,5},{5,6},{6,7},{8,9},{9,10},{10,11},{11... | collective-permute-start | bytes 786440 | tf_op jit(solution)/shard_map/ppermute | solution.py:21
  162.1 42.6 %collective-permute-start.12 = (f32[2,2,384,128]{3,2,1,0:T(8,128)}, f32[2,2,384,128]{3,2,1,0:T(8,128)S(1)}, u32[]{:S(2)}, u32[]{:S(2)}) collective-permute-start(f32[2,2,384,128]{3,2,1,0:T(8,128)} %get-tuple-element.27), channel_id=1, source_target_pairs={{0,1},{1,2},{2,3},{3,4},{4,5},{5,6},{6,7},{8,9},{9,10},{10,11},{11... | collective-permute-start | bytes 2359304 | tf_op jit(solution)/shard_map/ppermute | solution.py:21
  166.9 37.8 %collective-permute-start.14 = (f32[2,2,384,128]{3,2,1,0:T(8,128)}, f32[2,2,384,128]{3,2,1,0:T(8,128)S(1)}, u32[]{:S(2)}, u32[]{:S(2)}) collective-permute-start(f32[2,2,384,128]{3,2,1,0:T(8,128)} %get-tuple-element.28), channel_id=1, source_target_pairs={{1,0},{2,1},{3,2},{4,3},{5,4},{6,5},{7,6},{9,8},{10,9},{11,10},{12... | collective-permute-start | bytes 2359304 | tf_op jit(solution)/shard_map/ppermute | solution.py:21
  168.9 35.9 %collective-permute-start.11 = (f32[2,2,128,384]{3,2,1,0:T(8,128)S(1)}, f32[2,2,128,384]{3,2,1,0:T(8,128)S(1)}, u32[]{:S(2)}, u32[]{:S(2)}) collective-permute-start(f32[2,2,128,384]{3,2,1,0:T(8,128)S(1)} %get-tuple-element.26), channel_id=1, source_target_pairs={{8,0},{16,8},{24,16},{9,1},{17,9},{25,17},{10,2},{18,10},{26,18},{... | collective-permute-start | bytes 2359304 | tf_op jit(solution)/shard_map/ppermute | solution.py:21
  170.2 34.5 %collective-permute-start.16 = (f32[2,2,128,256]{3,2,1,0:T(8,128)S(1)}, f32[2,2,128,256]{3,2,1,0:T(8,128)S(1)}, u32[]{:S(2)}, u32[]{:S(2)}) collective-permute-start(f32[2,2,128,256]{3,2,1,0:T(8,128)S(1)} %pad_maximum_fusion.2), channel_id=1, source_target_pairs={{8,0},{16,8},{24,16},{9,1},{17,9},{25,17},{10,2},{18,10},{26,18},{... | collective-permute-start | bytes 1572872 | tf_op jit(solution)/shard_map/ppermute | solution.py:21
  204.7 1.4 copy-start.11
  212.7 28.9 %collective-permute-start.17 = (f32[2,2,128,384]{3,2,1,0:T(8,128)S(1)}, f32[2,2,128,384]{3,2,1,0:T(8,128)S(1)}, u32[]{:S(2)}, u32[]{:S(2)}) collective-permute-start(f32[2,2,128,384]{3,2,1,0:T(8,128)S(1)} %get-tuple-element.30), channel_id=1, source_target_pairs={{0,8},{8,16},{16,24},{1,9},{9,17},{17,25},{2,10},{10,18},{18,26},{... | collective-permute-start | bytes 2359304 | tf_op jit(solution)/shard_map/ppermute | solution.py:21
  227.6 31.8 %collective-permute-start.18 = (f32[2,2,384,128]{3,2,1,0:T(8,128)S(1)}, f32[2,2,384,128]{3,2,1,0:T(8,128)S(1)}, u32[]{:S(2)}, u32[]{:S(2)}) collective-permute-start(f32[2,2,384,128]{3,2,1,0:T(8,128)S(1)} %get-tuple-element.31), channel_id=1, source_target_pairs={{0,1},{1,2},{2,3},{3,4},{4,5},{5,6},{6,7},{8,9},{9,10},{10,11},{11... | collective-permute-start | bytes 2359304 | tf_op jit(solution)/shard_map/ppermute | solution.py:21
  241.6 22.5 %collective-permute-start.19 = (f32[2,2,128,128]{3,2,1,0:T(8,128)S(1)}, f32[2,2,128,128]{3,2,1,0:T(8,128)S(1)}, u32[]{:S(2)}, u32[]{:S(2)}) collective-permute-start(f32[2,2,128,128]{3,2,1,0:T(8,128)S(1)} %slice_add_fusion), channel_id=1, source_target_pairs={{0,1},{1,2},{2,3},{3,4},{4,5},{5,6},{6,7},{8,9},{9,10},{10,11},{11... | collective-permute-start | bytes 786440 | tf_op jit(solution)/shard_map/ppermute | solution.py:21
  264.1 1.6 copy-start.1
  (3 other events, 2.9 us)
where the time goes:
time: 264 us; the launch traced here: 267 us
  waiting for transfers between devices  114 us (43%)
  starting transfers between devices  112 us (42%)
  Pallas kernels  31.9 us (12%)
  local copies, waits for them, and re-layouts  8.6 us (3%)
    ppermute x20, waiting for transfers between devices, shifted(): return lax.ppermute(array, axis, pairs)  114 us
    ppermute x20, starting transfers between devices, shifted(): return lax.ppermute(array, axis, pairs)  112 us
    pallas_call x3, Pallas kernels, windows(): pl.pallas_call(functools.partial(window_kernel, batch, first, last), out_...  30.4 us
  transfers between devices with their start and end apart: 20, of which 9 were waited for; matrix products, arithmetic and copies ran while one was open for 1% of the time, Pallas kernels for 0%

commit v1 on v0

--- a/solution.py
+++ b/solution.py
@@ -12,7 +12,7 @@
 
 BATCHES = 3
 STEP = 0.5
-VMEM_LIMIT = 50 * 1024 * 1024
+VMEM_LIMIT = 32 * 1024 * 1024
 
 
 def shifted(array, axis, by):
@@ -22,15 +22,27 @@
 
 
 def tables(length):
-    index = np.arange(length)
-    angle = (index[:, None] * index[None, :] % length) * (-2.0 * math.pi / length)
+    half = length // 2
+    index = np.arange(half)
     scale = 1.0 / math.sqrt(length)
-    re, im = np.cos(angle) * scale, np.sin(angle) * scale
-    right = np.block([[re, im], [-im, re]]).astype(np.float32)
-    high = right.astype(ml_dtypes.bfloat16)
-    low = (right - high.astype(np.float32)).astype(ml_dtypes.bfloat16)
-    stacked = np.concatenate([high, high, low], axis=0)
-    return stacked, np.ascontiguousarray(stacked.T)
+    lefts = []
+    for odd in range(2):
+        angle = ((2 * index[:, None] + odd) * index[None, :] % length) * (-2.0 * math.pi / length)
+        re, im = np.cos(angle) * scale, np.sin(angle) * scale
+        real = np.block([[re, -im], [im, re]]).astype(np.float32)
+        lefts.append(real)
+    out = []
+    for real in lefts + [m.T for m in lefts]:
+        high = real.astype(ml_dtypes.bfloat16)
+        low = (real - high.astype(np.float32)).astype(ml_dtypes.bfloat16)
+        out.append(np.concatenate([high, high, low], axis=1))
+    left = np.stack(out)
+    right = np.stack([np.concatenate([m[:, :length].T, m[:, length : 2 * length].T, m[:, 2 * length :].T]) for m in out])
+    pick = np.zeros((length, length), np.float32)
+    order = np.concatenate([np.arange(0, length, 2), np.arange(1, length, 2)])
+    pick[np.arange(length), order] = 1.0
+    pick = np.concatenate([pick] * 3, axis=1).astype(ml_dtypes.bfloat16)
+    return left, right, pick, np.ascontiguousarray(pick.T)
 
 
 def split(value):
@@ -39,26 +51,69 @@
     return high, low
 
 
+def on_rows(table, value):
+    high, low = split(value)
+    return jnp.dot(table, jnp.concatenate([high, low, high], axis=0), preferred_element_type=jnp.float32)
+
+
+def on_cols(value, table):
+    high, low = split(value)
+    return jnp.dot(jnp.concatenate([high, low, high], axis=1), table, preferred_element_type=jnp.float32)
+
+
+def halves(value, axis):
+    half = value.shape[axis] // 2
+    return (value[:half], value[half:]) if axis == 0 else (value[:, :half], value[:, half:])
+
+
+def forward_axis(re, im, axis, apply):
+    (ra, rb), (ia, ib) = halves(re, axis), halves(im, axis)
+    even = apply(0, jnp.concatenate([ra + rb, ia + ib], axis=axis))
+    odd = apply(1, jnp.concatenate([ra - rb, ia - ib], axis=axis))
+    (er, ei), (dr, di) = halves(even, axis), halves(odd, axis)
+    return jnp.concatenate([er, dr], axis=axis), jnp.concatenate([ei, di], axis=axis)
+
+
+def inverse_axis(re, im, axis, apply):
+    (er, dr), (ei, di) = halves(re, axis), halves(im, axis)
+    even = apply(2, jnp.concatenate([er, ei], axis=axis))
+    odd = apply(3, jnp.concatenate([dr, di], axis=axis))
+    (ra, ia), (rb, ib) = halves(even + odd, axis), halves(even - odd, axis)
+    return jnp.concatenate([ra, rb], axis=axis), jnp.concatenate([ia, ib], axis=axis)
+
+
 def forward(re, im, right_ref, left_ref):
-    n = re.shape[0]
-    (rh, rl), (ih, il) = split(re), split(im)
-    y = jnp.dot(
-        jnp.concatenate([rh, ih, rl, il, rh, ih], axis=1),
-        right_ref[...],
-        preferred_element_type=jnp.float32,
-    )
-    (rh, rl), (ih, il) = split(y[:, :n]), split(y[:, n:])
-    z = jnp.dot(
-        left_ref[...],
-        jnp.concatenate([rh, ih, rl, il, rh, ih], axis=0),
-        preferred_element_type=jnp.float32,
-    )
-    return z[:n], z[n:]
+    re, im = forward_axis(re, im, 1, lambda i, v: on_cols(v, right_ref[i]))
+    return forward_axis(re, im, 0, lambda i, v: on_rows(left_ref[i], v))
 
 
 def inverse(re, im, right_ref, left_ref):
-    out_im, out_re = forward(im, re, right_ref, left_ref)
-    return out_re, out_im
+    re, im = inverse_axis(re, im, 0, lambda i, v: on_rows(left_ref[i], v))
+    return inverse_axis(re, im, 1, lambda i, v: on_cols(v, right_ref[i]))
+
+
+def thirds(value):
+    high = value.astype(jnp.bfloat16)
+    value = value - high.astype(jnp.float32)
+    middle = value.astype(jnp.bfloat16)
+    low = (value - middle.astype(jnp.float32)).astype(jnp.bfloat16)
+    return [high, middle, low]
+
+
+def reorder_kernel(amplitude, prop, pick, pick_t, amplitude_out, prop_out):
+    def move(value):
+        rows = jnp.dot(pick[...], jnp.concatenate(thirds(value), axis=0), preferred_element_type=jnp.float32)
+        return jnp.dot(jnp.concatenate(thirds(rows), axis=1), pick_t[...], preferred_element_type=jnp.float32)
+
+    def each(source, target):
+        def step(i, carry):
+            target[i] = move(source[i])
+            return carry
+
+        lax.fori_loop(0, source.shape[0], step, 0)
+
+    each(amplitude, amplitude_out)
+    each(prop, prop_out)
 
 
 def window_kernel(batch, first, last, *refs):
@@ -198,7 +253,7 @@
     strip = win // 2
     rows, cols = transmission.shape[2:]
     wide = cols + strip
-    right_t, left_t = (jnp.asarray(t) for t in tables(win))
+    left_t, right_t, pick, pick_t = (jnp.asarray(t) for t in tables(win))
     prop = jnp.stack([jnp.cos(prop_phase), jnp.sin(prop_phase)])
     measured = amplitude[0, 0]
     keep = jnp.stack(
@@ -209,6 +264,21 @@
     )
     smem = pl.BlockSpec(memory_space=pltpu.SMEM)
     vmem = pl.BlockSpec(memory_space=pltpu.VMEM)
+    planes = amplitude.shape[2] + 2
+    measured, prop = pl.pallas_call(
+        reorder_kernel,
+        out_shape=(
+            jax.ShapeDtypeStruct(measured.shape, jnp.float32),
+            jax.ShapeDtypeStruct(prop.shape, jnp.float32),
+        ),
+        in_specs=[vmem] * 4,
+        out_specs=(vmem, vmem),
+        compiler_params=pltpu.CompilerParams(vmem_limit_bytes=VMEM_LIMIT // 2),
+        cost_estimate=pl.CostEstimate(
+            flops=planes * 12 * win**3, bytes_accessed=planes * 8 * win**2, transcendentals=0
+        ),
+        name="reorder",
+    )(measured, prop, pick, pick_t)
 
     def shape(r, c):
         return jax.ShapeDtypeStruct((2, 2, r, c), jnp.float32)

time: 264 us -> 219 us (0.83); the launches traced: 267 us -> 220 us
  starting transfers between devices: 112 us -> 62.5 us
    ppermute x20, starting transfers between devices: 112 us -> 62.5 us  [shifted(): return lax.ppermute(array, axis, pairs)]
    pallas_call x3, Pallas kernels: 30.4 us -> 25.4 us  [windows(): pl.pallas_call(functools.partial(window_kernel, batch, first, last), out_...]
    pallas_call x0 -> x1, Pallas kernels: none -> 3.65 us  [body(): pl.pallas_call(reorder_kernel, out_shape=(jax.ShapeDtypeStruct(measured.s...]
  transfers between devices with their start and end apart: 20 -> 20, of which waited for: 9 -> 11; matrix products, arithmetic and copies ran while one was open for 1% -> 1% of each run, Pallas kernels for 0% -> 2%
where the time goes in v1:
time: 219 us; the launch traced here: 220 us
  waiting for transfers between devices  116 us (53%)
  starting transfers between devices  62.5 us (29%)
  Pallas kernels  30.5 us (14%)
  local copies, waits for them, and re-layouts  9.26 us (4%)
    ppermute x20, waiting for transfers between devices, shifted(): return lax.ppermute(array, axis, pairs)  116 us
    ppermute x20, starting transfers between devices, shifted(): return lax.ppermute(array, axis, pairs)  62.5 us
    pallas_call x3, Pallas kernels, windows(): pl.pallas_call(functools.partial(window_kernel, batch, first, last), out_...  25.4 us
  transfers between devices with their start and end apart: 20, of which 11 were waited for; matrix products, arithmetic and copies ran while one was open for 1% of the time, Pallas kernels for 2%

profile of v1, /device:TPU:16, one launch (start us, length us, event | category | flops | bytes accessed | tf_op | source)
XLA Modules:
  0.0 219.5 jit_solution(14796937353279474555)
XLA Ops:
  0.0 2.4 %slice.37 = f32[2,2,512,128]{3,2,1,0:T(8,128)} slice(f32[2,2,512,256]{3,2,1,0:T(8,128)} %refs_5_.1), slice={[0:2], [0:2], [0:512], [0:128]} | slice | bytes 2097152 | tf_op jit(solution)/shard_map/slice | solution.py:314
  2.4 3.4 %collective-permute-start.1 = (f32[2,2,512,128]{3,2,1,0:T(8,128)}, f32[2,2,512,128]{3,2,1,0:T(8,128)S(1)}, u32[]{:S(2)}, u32[]{:S(2)}) collective-permute-start(f32[2,2,512,128]{3,2,1,0:T(8,128)} %slice.37), channel_id=1, source_target_pairs={{1,0},{2,1},{3,2},{4,3},{5,4},{6,5},{7,6},{9,8},{10,9},{11,10},{12... | collective-permute-start | bytes 3145736 | tf_op jit(solution)/shard_map/ppermute | solution.py:21
  8.0 2.0 cosine_bitcast_fusion
  10.0 19.6 %collective-permute-done.1.refs_7_ = f32[2,2,512,128]{3,2,1,0:T(8,128)S(1)} collective-permute-done((f32[2,2,512,128]{3,2,1,0:T(8,128)}, f32[2,2,512,128]{3,2,1,0:T(8,128)S(1)}, u32[]{:S(2)}, u32[]{:S(2)}) %collective-permute-start.1) | collective-permute-done | bytes 1048608 | tf_op jit(solution)/shard_map/ppermute | solution.py:21
  31.7 3.6 %reorder.1 = (f32[4,256,256]{2,1,0:T(8,128)S(1)}, f32[2,256,256]{2,1,0:T(8,128)S(1)}) custom-call(f32[4,256,256]{2,1,0:T(8,128)S(1)} %bitcast.7, f32[2,256,256]{2,1,0:T(8,128)S(1)} %pad_maximum_fusion.prop, bf16[256,768]{1,0:T(8,128)(2,1)S(1)} %copy-done.11, bf16[768,256]{1,0:T(8,128)(2,1)S(1)} %copy-done.10), custom_call_target="tpu_custom_call" | custom-call | flops 1207959552 | bytes 3145728 | tf_op jit(solution)/shard_map/reorder/pallas_call | solution.py:268
  35.5 17.0 %windows0.1 = (f32[2,2,640,384]{3,2,1,0:T(8,128)S(1)}, f32[2,2,128,384]{3,2,1,0:T(8,128)S(1)}, f32[2,2,128,384]{3,2,1,0:T(8,128)S(1)}, f32[2,2,384,128]{3,2,1,0:T(8,128)S(1)}, f32[2,2,384,128]{3,2,1,0:T(8,128)S(1)}) custom-call(s32[1,1]{1,0:T(1,128)S(6)} %copy.13.refs_0_, s32[1,1,4]{2,1,0:T(1,128)S(1)} %copy-done.6, s32[1,1,4]{2,1,0:T(1,128)S(1)} %copy-done.7, ...), custom_call_target="tpu_custom_call" | custom-call | tf_op jit(solution)/shard_map/windows0/pallas_call | solution.py:298
  52.5 1.9 copy-done.4
  55.7 1.8 collective-permute-done.3.refs_6_
  57.6 1.9 collective-permute-start.8
  59.5 3.9 %collective-permute-start.6 = (f32[2,2,128,128]{3,2,1,0:T(8,128)S(1)}, f32[2,2,128,128]{3,2,1,0:T(8,128)S(1)}, u32[]{:S(2)}, u32[]{:S(2)}) collective-permute-start(f32[2,2,128,128]{3,2,1,0:T(8,128)S(1)} %get-tuple-element.40), channel_id=1, source_target_pairs={{0,1},{1,2},{2,3},{3,4},{4,5},{5,6},{6,7},{8,9},{9,10},{10,11},{11... | collective-permute-start | bytes 786440 | tf_op jit(solution)/shard_map/ppermute | solution.py:21
  63.5 1.9 collective-permute-start.5
  65.4 4.8 %collective-permute-start.7 = (f32[2,2,384,128]{3,2,1,0:T(8,128)S(1)}, f32[2,2,384,128]{3,2,1,0:T(8,128)S(1)}, u32[]{:S(2)}, u32[]{:S(2)}) collective-permute-start(f32[2,2,384,128]{3,2,1,0:T(8,128)S(1)} %get-tuple-element.27), channel_id=1, source_target_pairs={{1,0},{2,1},{3,2},{4,3},{5,4},{6,5},{7,6},{9,8},{10,9},{11,10},{12... | collective-permute-start | bytes 2359304 | tf_op jit(solution)/shard_map/ppermute | solution.py:21
  71.5 19.6 %collective-permute-done.8.refs_11_ = f32[2,2,128,128]{3,2,1,0:T(8,128)S(1)} collective-permute-done((f32[2,2,128,128]{3,2,1,0:T(8,128)S(1)}, f32[2,2,128,128]{3,2,1,0:T(8,128)S(1)}, u32[]{:S(2)}, u32[]{:S(2)}) %collective-permute-start.8) | collective-permute-done | bytes 262176 | tf_op jit(solution)/shard_map/ppermute | solution.py:21
  92.6 11.9 %collective-permute-done.5.refs_8_ = f32[2,2,384,128]{3,2,1,0:T(8,128)S(1)} collective-permute-done((f32[2,2,384,128]{3,2,1,0:T(8,128)S(1)}, f32[2,2,384,128]{3,2,1,0:T(8,128)S(1)}, u32[]{:S(2)}, u32[]{:S(2)}) %collective-permute-start.5) | collective-permute-done | bytes 786464 | tf_op jit(solution)/shard_map/ppermute | solution.py:21
  104.5 2.9 %collective-permute-done.7.refs_10_ = f32[2,2,384,128]{3,2,1,0:T(8,128)S(1)} collective-permute-done((f32[2,2,384,128]{3,2,1,0:T(8,128)S(1)}, f32[2,2,384,128]{3,2,1,0:T(8,128)S(1)}, u32[]{:S(2)}, u32[]{:S(2)}) %collective-permute-start.7) | collective-permute-done | bytes 786464 | tf_op jit(solution)/shard_map/ppermute | solution.py:21
  107.4 2.1 copy-done.5
  109.5 6.7 %windows1.1 = (f32[2,2,640,384]{3,2,1,0:T(8,128)S(1)}, f32[2,2,128,384]{3,2,1,0:T(8,128)S(1)}, f32[2,2,128,384]{3,2,1,0:T(8,128)S(1)}, f32[2,2,384,128]{3,2,1,0:T(8,128)S(1)}, f32[2,2,384,128]{3,2,1,0:T(8,128)S(1)}) custom-call(s32[1,1]{1,0:T(1,128)S(6)} %copy.13.refs_0_, s32[1,1,4]{2,1,0:T(1,128)S(1)} %copy-done.6, s32[1,1,4]{2,1,0:T(1,128)S(1)} %copy-done.7, ...), custom_call_target="tpu_custom_call" | custom-call | tf_op jit(solution)/shard_map/windows1/pallas_call | solution.py:298
  116.3 1.6 collective-permute-start.10
  117.9 1.8 collective-permute-done.10.refs_6_
  119.8 8.7 %collective-permute-start.15 = (f32[2,2,128,128]{3,2,1,0:T(8,128)S(1)}, f32[2,2,128,128]{3,2,1,0:T(8,128)S(1)}, u32[]{:S(2)}, u32[]{:S(2)}) collective-permute-start(f32[2,2,128,128]{3,2,1,0:T(8,128)S(1)} %get-tuple-element.37), channel_id=1, source_target_pairs={{1,0},{2,1},{3,2},{4,3},{5,4},{6,5},{7,6},{9,8},{10,9},{11,10},{12... | collective-permute-start | bytes 786440 | tf_op jit(solution)/shard_map/ppermute | solution.py:21
  128.4 1.9 collective-permute-start.13
  130.3 1.9 collective-permute-start.12
  132.3 4.8 %collective-permute-start.14 = (f32[2,2,384,128]{3,2,1,0:T(8,128)S(1)}, f32[2,2,384,128]{3,2,1,0:T(8,128)S(1)}, u32[]{:S(2)}, u32[]{:S(2)}) collective-permute-start(f32[2,2,384,128]{3,2,1,0:T(8,128)S(1)} %get-tuple-element.32), channel_id=1, source_target_pairs={{1,0},{2,1},{3,2},{4,3},{5,4},{6,5},{7,6},{9,8},{10,9},{11,10},{12... | collective-permute-start | bytes 2359304 | tf_op jit(solution)/shard_map/ppermute | solution.py:21
  138.4 8.7 %collective-permute-done.13.refs_9_ = f32[2,2,128,128]{3,2,1,0:T(8,128)S(1)} collective-permute-done((f32[2,2,128,128]{3,2,1,0:T(8,128)S(1)}, f32[2,2,128,128]{3,2,1,0:T(8,128)S(1)}, u32[]{:S(2)}, u32[]{:S(2)}) %collective-permute-start.13) | collective-permute-done | bytes 262176 | tf_op jit(solution)/shard_map/ppermute | solution.py:21
  148.4 23.9 %collective-permute-done.12.refs_8_ = f32[2,2,384,128]{3,2,1,0:T(8,128)S(1)} collective-permute-done((f32[2,2,384,128]{3,2,1,0:T(8,128)S(1)}, f32[2,2,384,128]{3,2,1,0:T(8,128)S(1)}, u32[]{:S(2)}, u32[]{:S(2)}) %collective-permute-start.12) | collective-permute-done | bytes 786464 | tf_op jit(solution)/shard_map/ppermute | solution.py:21
  172.4 1.6 collective-permute-done.14.refs_10_
  174.0 1.6 windows2.1
  175.6 14.5 %collective-permute-start.17 = (f32[2,2,128,384]{3,2,1,0:T(8,128)S(1)}, f32[2,2,128,384]{3,2,1,0:T(8,128)S(1)}, u32[]{:S(2)}, u32[]{:S(2)}) collective-permute-start(f32[2,2,128,384]{3,2,1,0:T(8,128)S(1)} %get-tuple-element.34), channel_id=1, source_target_pairs={{0,8},{8,16},{16,24},{1,9},{9,17},{17,25},{2,10},{10,18},{18,26},{... | collective-permute-start | bytes 2359304 | tf_op jit(solution)/shard_map/ppermute | solution.py:21
  190.2 1.9 collective-permute-start.18
  192.1 1.9 collective-permute-start.19
  194.1 19.3 %collective-permute-done.18.fr_one = f32[2,2,384,128]{3,2,1,0:T(8,128)S(1)} collective-permute-done((f32[2,2,384,128]{3,2,1,0:T(8,128)S(1)}, f32[2,2,384,128]{3,2,1,0:T(8,128)S(1)}, u32[]{:S(2)}, u32[]{:S(2)}) %collective-permute-start.18) | collective-permute-done | bytes 786464 | tf_op jit(solution)/shard_map/ppermute | solution.py:21
  213.4 4.6 %collective-permute-done.19.fr_two = f32[2,2,128,128]{3,2,1,0:T(8,128)S(1)} collective-permute-done((f32[2,2,128,128]{3,2,1,0:T(8,128)S(1)}, f32[2,2,128,128]{3,2,1,0:T(8,128)S(1)}, u32[]{:S(2)}, u32[]{:S(2)}) %collective-permute-start.19) | collective-permute-done | bytes 262176 | tf_op jit(solution)/shard_map/ppermute | solution.py:21
  (48 shorter events, 12.0 us)
Async XLA Ops:
  0.0 5.8 %copy-start.2 = (f32[2,2,512,256]{3,2,1,0:T(8,128)S(1)}, f32[2,2,512,256]{3,2,1,0:T(8,128)}, u32[]{:S(2)}) copy-start(f32[2,2,512,256]{3,2,1,0:T(8,128)} %refs_5_.1) | copy-start | bytes 6291460
  2.4 29.2 %copy-start.10 = (bf16[768,256]{1,0:T(8,128)(2,1)S(1)}, bf16[768,256]{1,0:T(8,128)(2,1)}, u32[]{:S(2)}) copy-start(bf16[768,256]{1,0:T(8,128)(2,1)} %constant.23.clone.pick_t) | copy-start | bytes 1179652
  2.4 27.1 %collective-permute-start.1 = (f32[2,2,512,128]{3,2,1,0:T(8,128)}, f32[2,2,512,128]{3,2,1,0:T(8,128)S(1)}, u32[]{:S(2)}, u32[]{:S(2)}) collective-permute-start(f32[2,2,512,128]{3,2,1,0:T(8,128)} %slice.37), channel_id=1, source_target_pairs={{1,0},{2,1},{3,2},{4,3},{5,4},{6,5},{7,6},{9,8},{10,9},{11,10},{12... | collective-permute-start | bytes 3145736 | tf_op jit(solution)/shard_map/ppermute | solution.py:21
  6.7 28.7 %collective-permute-start = (f32[2,2,128,256]{3,2,1,0:T(8,128)}, f32[2,2,128,256]{3,2,1,0:T(8,128)}, u32[]{:S(2)}, u32[]{:S(2)}) collective-permute-start(f32[2,2,128,256]{3,2,1,0:T(8,128)} %slice.36), channel_id=1, source_target_pairs={{8,0},{16,8},{24,16},{9,1},{17,9},{25,17},{10,2},{18,10},{26,18},{... | collective-permute-start | bytes 1572872 | tf_op jit(solution)/shard_map/ppermute | solution.py:21
  8.0 23.7 %copy-start.9 = (f32[1,1,4,256,256]{4,3,2,1,0:T(8,128)S(1)}, f32[1,1,4,256,256]{4,3,2,1,0:T(8,128)}, u32[]{:S(2)}) copy-start(f32[1,1,4,256,256]{4,3,2,1,0:T(8,128)} %param.15) | copy-start | bytes 3145732
  8.0 23.7 %copy-start.11 = (bf16[256,768]{1,0:T(8,128)(2,1)S(1)}, bf16[256,768]{1,0:T(8,128)(2,1)}, u32[]{:S(2)}) copy-start(bf16[256,768]{1,0:T(8,128)(2,1)} %constant.22.clone.pick) | copy-start | bytes 1179652
  29.6 5.8 %collective-permute-start.2 = (f32[2,2,128,128]{3,2,1,0:T(8,128)S(1)}, f32[2,2,128,128]{3,2,1,0:T(8,128)S(1)}, u32[]{:S(2)}, u32[]{:S(2)}) collective-permute-start(f32[2,2,128,128]{3,2,1,0:T(8,128)S(1)} %slice.48), channel_id=1, source_target_pairs={{8,0},{16,8},{24,16},{9,1},{17,9},{25,17},{10,2},{18,10},{26,18},{... | collective-permute-start | bytes 786440 | tf_op jit(solution)/shard_map/ppermute | solution.py:21
  31.7 3.8 %copy-start = (bf16[4,768,256]{2,1,0:T(8,128)(2,1)S(1)}, bf16[4,768,256]{2,1,0:T(8,128)(2,1)}, u32[]{:S(2)}) copy-start(bf16[4,768,256]{2,1,0:T(8,128)(2,1)} %constant.21.clone.refs_12_.refs_16_) | copy-start | bytes 4718596
  31.7 3.7 %copy-start.1 = (bf16[4,256,768]{2,1,0:T(8,128)(2,1)S(1)}, bf16[4,256,768]{2,1,0:T(8,128)(2,1)}, u32[]{:S(2)}) copy-start(bf16[4,256,768]{2,1,0:T(8,128)(2,1)} %constant.20.clone.refs_13_.refs_17_) | copy-start | bytes 4718596
  31.7 3.7 %copy-start.3 = (f32[2,256,256]{2,1,0:T(8,128)S(1)}, f32[2,256,256]{2,1,0:T(8,128)}, u32[]{:S(2)}) copy-start(f32[2,256,256]{2,1,0:T(8,128)} %refs_13_.4) | copy-start | bytes 1572868
  31.7 3.7 %copy-start.6 = (s32[1,1,4]{2,1,0:T(1,128)S(1)}, s32[1,1,4]{2,1,0:T(1,128)}, u32[]{:S(2)}) copy-start(s32[1,1,4]{2,1,0:T(1,128)} %refs_1_.5) | copy-start | bytes 52
  31.7 3.7 %copy-start.7 = (s32[1,1,4]{2,1,0:T(1,128)S(1)}, s32[1,1,4]{2,1,0:T(1,128)}, u32[]{:S(2)}) copy-start(s32[1,1,4]{2,1,0:T(1,128)} %refs_2_.5) | copy-start | bytes 52
  31.7 3.7 %copy-start.8 = (s32[1,1,4]{2,1,0:T(1,128)S(1)}, s32[1,1,4]{2,1,0:T(1,128)}, u32[]{:S(2)}) copy-start(s32[1,1,4]{2,1,0:T(1,128)} %refs_3_.5) | copy-start | bytes 52
  52.5 1.9 copy-start.4
  54.4 3.2 %collective-permute-start.3 = (f32[2,2,128,384]{3,2,1,0:T(8,128)S(1)}, f32[2,2,128,384]{3,2,1,0:T(8,128)S(1)}, u32[]{:S(2)}, u32[]{:S(2)}) collective-permute-start(f32[2,2,128,384]{3,2,1,0:T(8,128)S(1)} %get-tuple-element.24), channel_id=1, source_target_pairs={{0,8},{8,16},{16,24},{1,9},{9,17},{17,25},{2,10},{10,18},{18,26},{... | collective-permute-start | bytes 2359304 | tf_op jit(solution)/shard_map/ppermute | solution.py:21
  57.6 33.5 %collective-permute-start.8 = (f32[2,2,128,128]{3,2,1,0:T(8,128)S(1)}, f32[2,2,128,128]{3,2,1,0:T(8,128)S(1)}, u32[]{:S(2)}, u32[]{:S(2)}) collective-permute-start(f32[2,2,128,128]{3,2,1,0:T(8,128)S(1)} %get-tuple-element.39), channel_id=1, source_target_pairs={{1,0},{2,1},{3,2},{4,3},{5,4},{6,5},{7,6},{9,8},{10,9},{11,10},{12... | collective-permute-start | bytes 786440 | tf_op jit(solution)/shard_map/ppermute | solution.py:21
  59.5 31.6 %collective-permute-start.6 = (f32[2,2,128,128]{3,2,1,0:T(8,128)S(1)}, f32[2,2,128,128]{3,2,1,0:T(8,128)S(1)}, u32[]{:S(2)}, u32[]{:S(2)}) collective-permute-start(f32[2,2,128,128]{3,2,1,0:T(8,128)S(1)} %get-tuple-element.40), channel_id=1, source_target_pairs={{0,1},{1,2},{2,3},{3,4},{4,5},{5,6},{6,7},{8,9},{9,10},{10,11},{11... | collective-permute-start | bytes 786440 | tf_op jit(solution)/shard_map/ppermute | solution.py:21
  63.5 41.1 %collective-permute-start.5 = (f32[2,2,384,128]{3,2,1,0:T(8,128)S(1)}, f32[2,2,384,128]{3,2,1,0:T(8,128)S(1)}, u32[]{:S(2)}, u32[]{:S(2)}) collective-permute-start(f32[2,2,384,128]{3,2,1,0:T(8,128)S(1)} %get-tuple-element.26), channel_id=1, source_target_pairs={{0,1},{1,2},{2,3},{3,4},{4,5},{5,6},{6,7},{8,9},{9,10},{10,11},{11... | collective-permute-start | bytes 2359304 | tf_op jit(solution)/shard_map/ppermute | solution.py:21
  65.4 42.0 %collective-permute-start.7 = (f32[2,2,384,128]{3,2,1,0:T(8,128)S(1)}, f32[2,2,384,128]{3,2,1,0:T(8,128)S(1)}, u32[]{:S(2)}, u32[]{:S(2)}) collective-permute-start(f32[2,2,384,128]{3,2,1,0:T(8,128)S(1)} %get-tuple-element.27), channel_id=1, source_target_pairs={{1,0},{2,1},{3,2},{4,3},{5,4},{6,5},{7,6},{9,8},{10,9},{11,10},{12... | collective-permute-start | bytes 2359304 | tf_op jit(solution)/shard_map/ppermute | solution.py:21
  70.2 37.2 %collective-permute-start.4 = (f32[2,2,128,384]{3,2,1,0:T(8,128)S(1)}, f32[2,2,128,384]{3,2,1,0:T(8,128)S(1)}, u32[]{:S(2)}, u32[]{:S(2)}) collective-permute-start(f32[2,2,128,384]{3,2,1,0:T(8,128)S(1)} %get-tuple-element.25), channel_id=1, source_target_pairs={{8,0},{16,8},{24,16},{9,1},{17,9},{25,17},{10,2},{18,10},{26,18},{... | collective-permute-start | bytes 2359304 | tf_op jit(solution)/shard_map/ppermute | solution.py:21
  91.2 16.3 %collective-permute-start.9 = (f32[2,2,128,256]{3,2,1,0:T(8,128)S(1)}, f32[2,2,128,256]{3,2,1,0:T(8,128)S(1)}, u32[]{:S(2)}, u32[]{:S(2)}) collective-permute-start(f32[2,2,128,256]{3,2,1,0:T(8,128)S(1)} %pad_maximum_fusion.1), channel_id=1, source_target_pairs={{8,0},{16,8},{24,16},{9,1},{17,9},{25,17},{10,2},{18,10},{26,18},{... | collective-permute-start | bytes 1572872 | tf_op jit(solution)/shard_map/ppermute | solution.py:21
  107.4 2.1 copy-start.5
  116.3 3.4 %collective-permute-start.10 = (f32[2,2,128,384]{3,2,1,0:T(8,128)S(1)}, f32[2,2,128,384]{3,2,1,0:T(8,128)S(1)}, u32[]{:S(2)}, u32[]{:S(2)}) collective-permute-start(f32[2,2,128,384]{3,2,1,0:T(8,128)S(1)} %get-tuple-element.29), channel_id=1, source_target_pairs={{0,8},{8,16},{16,24},{1,9},{9,17},{17,25},{2,10},{10,18},{18,26},{... | collective-permute-start | bytes 2359304 | tf_op jit(solution)/shard_map/ppermute | solution.py:21
  119.8 18.7 %collective-permute-start.15 = (f32[2,2,128,128]{3,2,1,0:T(8,128)S(1)}, f32[2,2,128,128]{3,2,1,0:T(8,128)S(1)}, u32[]{:S(2)}, u32[]{:S(2)}) collective-permute-start(f32[2,2,128,128]{3,2,1,0:T(8,128)S(1)} %get-tuple-element.37), channel_id=1, source_target_pairs={{1,0},{2,1},{3,2},{4,3},{5,4},{6,5},{7,6},{9,8},{10,9},{11,10},{12... | collective-permute-start | bytes 786440 | tf_op jit(solution)/shard_map/ppermute | solution.py:21
  128.4 18.7 %collective-permute-start.13 = (f32[2,2,128,128]{3,2,1,0:T(8,128)S(1)}, f32[2,2,128,128]{3,2,1,0:T(8,128)S(1)}, u32[]{:S(2)}, u32[]{:S(2)}) collective-permute-start(f32[2,2,128,128]{3,2,1,0:T(8,128)S(1)} %get-tuple-element.38), channel_id=1, source_target_pairs={{0,1},{1,2},{2,3},{3,4},{4,5},{5,6},{6,7},{8,9},{9,10},{10,11},{11... | collective-permute-start | bytes 786440 | tf_op jit(solution)/shard_map/ppermute | solution.py:21
  130.3 42.0 %collective-permute-start.12 = (f32[2,2,384,128]{3,2,1,0:T(8,128)S(1)}, f32[2,2,384,128]{3,2,1,0:T(8,128)S(1)}, u32[]{:S(2)}, u32[]{:S(2)}) collective-permute-start(f32[2,2,384,128]{3,2,1,0:T(8,128)S(1)} %get-tuple-element.31), channel_id=1, source_target_pairs={{0,1},{1,2},{2,3},{3,4},{4,5},{5,6},{6,7},{8,9},{9,10},{10,11},{11... | collective-permute-start | bytes 2359304 | tf_op jit(solution)/shard_map/ppermute | solution.py:21
  132.3 41.7 %collective-permute-start.14 = (f32[2,2,384,128]{3,2,1,0:T(8,128)S(1)}, f32[2,2,384,128]{3,2,1,0:T(8,128)S(1)}, u32[]{:S(2)}, u32[]{:S(2)}) collective-permute-start(f32[2,2,384,128]{3,2,1,0:T(8,128)S(1)} %get-tuple-element.32), channel_id=1, source_target_pairs={{1,0},{2,1},{3,2},{4,3},{5,4},{6,5},{7,6},{9,8},{10,9},{11,10},{12... | collective-permute-start | bytes 2359304 | tf_op jit(solution)/shard_map/ppermute | solution.py:21
  137.1 36.9 %collective-permute-start.11 = (f32[2,2,128,384]{3,2,1,0:T(8,128)S(1)}, f32[2,2,128,384]{3,2,1,0:T(8,128)S(1)}, u32[]{:S(2)}, u32[]{:S(2)}) collective-permute-start(f32[2,2,128,384]{3,2,1,0:T(8,128)S(1)} %get-tuple-element.30), channel_id=1, source_target_pairs={{8,0},{16,8},{24,16},{9,1},{17,9},{25,17},{10,2},{18,10},{26,18},{... | collective-permute-start | bytes 2359304 | tf_op jit(solution)/shard_map/ppermute | solution.py:21
  147.1 26.9 %collective-permute-start.16 = (f32[2,2,128,256]{3,2,1,0:T(8,128)S(1)}, f32[2,2,128,256]{3,2,1,0:T(8,128)S(1)}, u32[]{:S(2)}, u32[]{:S(2)}) collective-permute-start(f32[2,2,128,256]{3,2,1,0:T(8,128)S(1)} %pad_maximum_fusion.2), channel_id=1, source_target_pairs={{8,0},{16,8},{24,16},{9,1},{17,9},{25,17},{10,2},{18,10},{26,18},{... | collective-permute-start | bytes 1572872 | tf_op jit(solution)/shard_map/ppermute | solution.py:21
  175.6 16.5 %collective-permute-start.17 = (f32[2,2,128,384]{3,2,1,0:T(8,128)S(1)}, f32[2,2,128,384]{3,2,1,0:T(8,128)S(1)}, u32[]{:S(2)}, u32[]{:S(2)}) collective-permute-start(f32[2,2,128,384]{3,2,1,0:T(8,128)S(1)} %get-tuple-element.34), channel_id=1, source_target_pairs={{0,8},{8,16},{16,24},{1,9},{9,17},{17,25},{2,10},{10,18},{18,26},{... | collective-permute-start | bytes 2359304 | tf_op jit(solution)/shard_map/ppermute | solution.py:21
  190.2 23.2 %collective-permute-start.18 = (f32[2,2,384,128]{3,2,1,0:T(8,128)S(1)}, f32[2,2,384,128]{3,2,1,0:T(8,128)S(1)}, u32[]{:S(2)}, u32[]{:S(2)}) collective-permute-start(f32[2,2,384,128]{3,2,1,0:T(8,128)S(1)} %get-tuple-element.35), channel_id=1, source_target_pairs={{0,1},{1,2},{2,3},{3,4},{4,5},{5,6},{6,7},{8,9},{9,10},{10,11},{11... | collective-permute-start | bytes 2359304 | tf_op jit(solution)/shard_map/ppermute | solution.py:21
  192.1 25.8 %collective-permute-start.19 = (f32[2,2,128,128]{3,2,1,0:T(8,128)S(1)}, f32[2,2,128,128]{3,2,1,0:T(8,128)S(1)}, u32[]{:S(2)}, u32[]{:S(2)}) collective-permute-start(f32[2,2,128,128]{3,2,1,0:T(8,128)S(1)} %slice_add_fusion), channel_id=1, source_target_pairs={{0,1},{1,2},{2,3},{3,4},{4,5},{5,6},{6,7},{8,9},{9,10},{10,11},{11... | collective-permute-start | bytes 786440 | tf_op jit(solution)/shard_map/ppermute | solution.py:21

commit v2 on v1

--- a/solution.py
+++ b/solution.py
@@ -118,7 +118,7 @@
 
 def window_kernel(batch, first, last, *refs):
     count, row_off, col_off, which, keep = refs[:5]
-    n_in = 4 if first else 8
+    n_in = 5 if first else 9
     pieces = refs[5 : 5 + n_in]
     rest = refs[5 + n_in :]
     probe, prop, amplitude, right_t, left_t = rest[:5]
@@ -135,15 +135,16 @@
     slots = amplitude.shape[0]
 
     if first:
-        current, below, side, corner = pieces
+        current, below, side_top, side_rest, corner = pieces
         for a in range(2):
             for b in range(2):
                 ext[a, b, :rows, :cols] = current[a, b]
                 ext[a, b, rows : rows + strip, :cols] = below[a, b]
-                ext[a, b, :rows, cols:] = side[a, b]
+                ext[a, b, :strip, cols:] = side_top[a, b]
+                ext[a, b, strip:rows, cols:] = side_rest[a, b]
                 ext[a, b, rows : rows + strip, cols:] = corner[a, b]
     else:
-        old, from_up, from_down, fr_one, fr_two, fl_one, fl_two, corner = pieces
+        old, from_up, from_down, fr_one, fr_two, fl_one, fl_two, corner_near, corner_far = pieces
         keep_row = keep[0].astype(jnp.float32)
         keep_col = keep[1].astype(jnp.float32)
         for a in range(2):
@@ -158,13 +159,13 @@
                 ext[a, b, strip:rows, cols:] = (old[a, b, strip:rows, cols:] + fl_one[a, b]) * keep_col
                 bottom = pl.ds(rows, strip)
                 ext[a, b, bottom, :strip] = (
-                    old[a, b, bottom, :strip] + from_down[a, b, :, :strip] + corner[a, b, :, :strip]
+                    old[a, b, bottom, :strip] + from_down[a, b, :, :strip] + corner_near[a, b]
                 ) * keep_row
                 ext[a, b, bottom, strip:cols] = (
                     old[a, b, bottom, strip:cols] + from_down[a, b, :, strip:cols]
                 ) * keep_row
                 ext[a, b, bottom, cols:] = (
-                    old[a, b, bottom, cols:] + from_down[a, b, :, cols:] + corner[a, b, :, strip:]
+                    old[a, b, bottom, cols:] + from_down[a, b, :, cols:] + corner_far[a, b]
                 ) * (keep_row * keep_col)
     for a in range(2):
         for b in range(2):
@@ -233,6 +234,102 @@
                 left_one[a, b] = delta[a, b, strip:rows, :strip]
             down[a, b] = delta[a, b, rows : rows + strip]
             right_one[a, b] = delta[a, b, strip:rows, cols:]
+
+
+def exchange_kernel(last, *refs):
+    if last:
+        down, right_one, right_two, from_up, fr_one, fr_two, send_right, send, recv = refs
+        strip = right_two.shape[3]
+    else:
+        down, up, right_one, left_one = refs[:4]
+        from_up, from_down, fr_one, fr_two, fl_one, fl_two, corner_near, corner_far = refs[4:12]
+        send_right, send_left, send, recv = refs[12:]
+        strip = right_one.shape[3]
+    cols = down.shape[3] - strip
+    row, col = lax.axis_index("row"), lax.axis_index("col")
+    has_up, has_down = row > 0, row < lax.axis_size("row") - 1
+    has_left, has_right = col > 0, col < lax.axis_size("col") - 1
+    to_up, to_down, to_left, to_right = (row - 1, col), (row + 1, col), (row, col - 1), (row, col + 1)
+
+    def copy(index, source, target, device):
+        return pltpu.make_async_remote_copy(
+            src_ref=source,
+            dst_ref=target,
+            send_sem=send.at[index],
+            recv_sem=recv.at[index],
+            device_id=device,
+            device_id_type=pl.DeviceIdType.MESH,
+        )
+
+    copies = [
+        (copy(0, right_one, fr_one, to_right), has_right, has_left, fr_one),
+        (copy(1, down, from_up, to_down), has_down, has_up, from_up),
+        (copy(2, send_right, fr_two, to_right), has_right, has_left, fr_two),
+    ]
+    if not last:
+        copies += [
+            (copy(3, left_one, fl_one, to_left), has_left, has_right, fl_one),
+            (copy(4, up, from_down, to_up), has_up, has_down, from_down),
+            (copy(5, send_left, fl_two, to_left), has_left, has_right, fl_two),
+            (copy(6, fr_two, corner_near, to_up), has_up, has_down, corner_near),
+            (copy(7, fl_two, corner_far, to_up), has_up, has_down, corner_far),
+        ]
+
+    def start(index):
+        @pl.when(copies[index][1])
+        def _():
+            copies[index][0].start()
+
+    def arrive(index):
+        @pl.when(copies[index][2])
+        def _():
+            copies[index][0].wait_recv()
+
+    for _, _, comes, target in copies:
+
+        @pl.when(jnp.logical_not(comes))
+        def _(target=target):
+            target[...] = jnp.zeros(target.shape, jnp.float32)
+
+    barrier = pltpu.get_barrier_semaphore()
+    sides = ((has_up, to_up), (has_down, to_down), (has_left, to_left), (has_right, to_right))
+    for there, device in sides:
+
+        @pl.when(there)
+        def _(device=device):
+            pl.semaphore_signal(barrier, inc=1, device_id=device, device_id_type=pl.DeviceIdType.MESH)
+
+    pl.semaphore_wait(barrier, sum(there.astype(jnp.int32) for there, _ in sides))
+
+    start(1)
+    start(0)
+    if not last:
+        start(3)
+        start(4)
+    arrive(1)
+    if last:
+        send_right[...] = right_two[...] + from_up[:, :, :, cols:]
+        start(2)
+        arrive(2)
+    else:
+        send_right[...] = up[:, :, :, cols:] + from_up[:, :, :, cols:]
+        send_left[...] = up[:, :, :, :strip] + from_up[:, :, :, :strip]
+        start(2)
+        start(5)
+        arrive(2)
+        start(6)
+        arrive(5)
+        start(7)
+        arrive(3)
+        arrive(4)
+        arrive(6)
+        arrive(7)
+    arrive(0)
+    for one, goes, _, _ in copies:
+
+        @pl.when(goes)
+        def _(one=one):
+            one.wait_send()
 
 
 def finish_kernel(base, from_up, fr_one, fr_two, out):
@@ -311,24 +408,37 @@
             probe, prop, measured, right_t, left_t,
         )
 
-    side = shifted(transmission[:, :, :, :strip], "col", -1)
+    def exchange(batch, pieces):
+        last = batch == BATCHES - 1
+        block, rest = shape(strip, strip), shape(rows - strip, strip)
+        if last:
+            outs = (shape(strip, wide), rest, block)
+        else:
+            outs = (shape(strip, wide), shape(strip, wide), rest, block, rest, block, block, block)
+        sends, copies = (1, 3) if last else (2, 8)
+        return pl.pallas_call(
+            functools.partial(exchange_kernel, last),
+            out_shape=outs,
+            in_specs=[vmem] * len(pieces),
+            out_specs=[vmem] * len(outs),
+            scratch_shapes=[pltpu.VMEM(block.shape, jnp.float32)] * sends
+            + [pltpu.SemaphoreType.DMA((copies,)), pltpu.SemaphoreType.DMA((copies,))],
+            compiler_params=pltpu.CompilerParams(
+                vmem_limit_bytes=VMEM_LIMIT // 2, collective_id=batch, has_side_effects=True
+            ),
+            name=f"exchange{batch}",
+        )(*pieces)
+
+    side_top = shifted(transmission[:, :, :strip, :strip], "col", -1)
+    side_rest = shifted(transmission[:, :, strip:, :strip], "col", -1)
     below = shifted(transmission[:, :, :strip, :], "row", -1)
-    corner = shifted(side[:, :, :strip, :], "row", -1)
-    pieces = (transmission, below, side, corner)
+    corner = shifted(side_top, "row", -1)
+    pieces = (transmission, below, side_top, side_rest, corner)
     for batch in range(BATCHES - 1):
-        base, down, up, right_one, left_one = windows(batch, pieces)
-        from_up = shifted(down, "row", 1)
-        from_down = shifted(up, "row", -1)
-        fr_one = shifted(right_one, "col", 1)
-        fl_one = shifted(left_one, "col", -1)
-        fr_two = shifted(up[..., cols:] + from_up[..., cols:], "col", 1)
-        fl_two = shifted(up[..., :strip] + from_up[..., :strip], "col", -1)
-        corner = shifted(jnp.concatenate([fr_two, fl_two], axis=3), "row", -1)
-        pieces = (base, from_up, from_down, fr_one, fr_two, fl_one, fl_two, corner)
-    base, down, right_one, right_two = windows(BATCHES - 1, pieces)
-    from_up = shifted(down, "row", 1)
-    fr_one = shifted(right_one, "col", 1)
-    fr_two = shifted(right_two + from_up[..., cols:], "col", 1)
+        base, *sent = windows(batch, pieces)
+        pieces = (base, *exchange(batch, sent))
+    base, *sent = windows(BATCHES - 1, pieces)
+    from_up, fr_one, fr_two = exchange(BATCHES - 1, sent)
     return pl.pallas_call(
         finish_kernel,
         out_shape=shape(rows, cols),

time: 219 us -> 201 us (0.918)
  Pallas kernels: 30.5 us -> 167 us
  waiting for transfers between devices: 116 us -> 14.5 us
  starting transfers between devices: 62.5 us -> 8.4 us
  local copies, waits for them, and re-layouts: 9.26 us -> 11.5 us
    pallas_call x0 -> x3, Pallas kernels: none -> 141 us  [exchange(): pl.pallas_call(functools.partial(exchange_kernel, last), out_shape=outs,...]
    ppermute x20 -> x4, waiting for transfers between devices: 116 us -> 14.5 us  [shifted(): return lax.ppermute(array, axis, pairs)]
    ppermute x20 -> x4, starting transfers between devices: 62.5 us -> 8.4 us  [shifted(): return lax.ppermute(array, axis, pairs)]
    pallas_call x3, Pallas kernels: 25.4 us -> 20 us  [windows(): pl.pallas_call(functools.partial(window_kernel, batch, first, last), out_...]
  transfers between devices with their start and end apart: 20 -> 4, of which waited for: 11 -> 1; matrix products, arithmetic and copies ran while one was open for 1% -> 3% of each run, Pallas kernels for 2% -> 2%
where the time goes in v2:
time: 201 us; the launch traced here: 202 us
  Pallas kernels  167 us (83%)
  waiting for transfers between devices  14.5 us (7%)
  local copies, waits for them, and re-layouts  11.5 us (6%)
  starting transfers between devices  8.4 us (4%)
    pallas_call x3, Pallas kernels, exchange(): pl.pallas_call(functools.partial(exchange_kernel, last), out_shape=outs,...  141 us
    pallas_call x3, Pallas kernels, windows(): pl.pallas_call(functools.partial(window_kernel, batch, first, last), out_...  20 us
    ppermute x4, waiting for transfers between devices, shifted(): return lax.ppermute(array, axis, pairs)  14.5 us
    ppermute x4, starting transfers between devices, shifted(): return lax.ppermute(array, axis, pairs)  8.4 us
  transfers between devices with their start and end apart: 4, of which 1 were waited for; matrix products, arithmetic and copies ran while one was open for 3% of the time, Pallas kernels for 2%

profile of v2, /device:TPU:16, one launch (start us, length us, event | category | flops | bytes accessed | tf_op | source)
XLA Modules:
  0.0 201.9 jit_solution(6641423730446484064)
XLA Ops:
  0.0 2.1 %slice.11 = f32[2,2,384,128]{3,2,1,0:T(8,128)} slice(f32[2,2,512,256]{3,2,1,0:T(8,128)} %refs_5_.1), slice={[0:2], [0:2], [128:512], [0:128]} | slice | bytes 1572864 | tf_op jit(solution)/shard_map/slice | solution.py:433
  2.1 3.4 %collective-permute-start.2 = (f32[2,2,384,128]{3,2,1,0:T(8,128)}, f32[2,2,384,128]{3,2,1,0:T(8,128)S(1)}, u32[]{:S(2)}, u32[]{:S(2)}) collective-permute-start(f32[2,2,384,128]{3,2,1,0:T(8,128)} %slice.11), channel_id=1, source_target_pairs={{1,0},{2,1},{3,2},{4,3},{5,4},{6,5},{7,6},{9,8},{10,9},{11,10},{12... | collective-permute-start | bytes 2359304 | tf_op jit(solution)/shard_map/ppermute | solution.py:21
  5.5 1.7 slice.10
  7.2 2.4 %collective-permute-start.1 = (f32[2,2,128,128]{3,2,1,0:T(8,128)}, f32[2,2,128,128]{3,2,1,0:T(8,128)S(1)}, u32[]{:S(2)}, u32[]{:S(2)}) collective-permute-start(f32[2,2,128,128]{3,2,1,0:T(8,128)} %slice.10), channel_id=1, source_target_pairs={{1,0},{2,1},{3,2},{4,3},{5,4},{6,5},{7,6},{9,8},{10,9},{11,10},{12... | collective-permute-start | bytes 786440 | tf_op jit(solution)/shard_map/ppermute | solution.py:21
  9.6 1.9 slice.9
  11.5 1.3 collective-permute-start
  12.8 0.0 copy-start.3
  12.8 1.9 cosine_bitcast_fusion
  14.7 14.5 %collective-permute-done.1.refs_7_ = f32[2,2,128,128]{3,2,1,0:T(8,128)S(1)} collective-permute-done((f32[2,2,128,128]{3,2,1,0:T(8,128)}, f32[2,2,128,128]{3,2,1,0:T(8,128)S(1)}, u32[]{:S(2)}, u32[]{:S(2)}) %collective-permute-start.1) | collective-permute-done | bytes 262176 | tf_op jit(solution)/shard_map/ppermute | solution.py:21
  29.2 1.3 collective-permute-start.3
  30.5 0.1 add_convert_fusion.refs_4_
  31.2 0.0 copy-start.2
  31.3 0.0 copy-done.11
  31.3 0.0 copy-done.12
  31.3 0.0 copy-start.13
  31.3 1.1 copy-done.13
  32.5 0.0 copy-start.10
  32.5 3.6 %reorder.1 = (f32[4,256,256]{2,1,0:T(8,128)S(1)}, f32[2,256,256]{2,1,0:T(8,128)S(1)}) custom-call(f32[4,256,256]{2,1,0:T(8,128)S(1)} %bitcast.7, f32[2,256,256]{2,1,0:T(8,128)S(1)} %pad_maximum_fusion.prop, bf16[256,768]{1,0:T(8,128)(2,1)S(1)} %copy-done.13, bf16[768,256]{1,0:T(8,128)(2,1)S(1)} %copy-done.12), custom_call_target="tpu_custom_call" | custom-call | flops 1207959552 | bytes 3145728 | tf_op jit(solution)/shard_map/reorder/pallas_call | solution.py:365
  36.1 0.0 collective-permute-done.3.refs_9_
  36.1 0.0 collective-permute-done.refs_6_
  36.2 0.8 copy-done.4
  37.0 0.0 collective-permute-done.2.refs_8_
  37.0 0.0 copy-done.2
  37.0 1.0 copy-done.5
  38.1 0.9 copy-done.7
  39.0 11.6 %windows0.1 = (f32[2,2,640,384]{3,2,1,0:T(8,128)S(1)}, f32[2,2,128,384]{3,2,1,0:T(8,128)S(1)}, f32[2,2,128,384]{3,2,1,0:T(8,128)S(1)}, f32[2,2,384,128]{3,2,1,0:T(8,128)S(1)}, f32[2,2,384,128]{3,2,1,0:T(8,128)S(1)}) custom-call(s32[1,1]{1,0:T(1,128)S(6)} %copy.13.refs_0_, s32[1,1,4]{2,1,0:T(1,128)S(1)} %copy-done.8, s32[1,1,4]{2,1,0:T(1,128)S(1)} %copy-done.9, ...), custom_call_target="tpu_custom_call" | custom-call | tf_op jit(solution)/shard_map/windows0/pallas_call | solution.py:395
  50.6 50.8 %exchange0.1 = (f32[2,2,128,384]{3,2,1,0:T(8,128)S(1)}, f32[2,2,128,384]{3,2,1,0:T(8,128)S(1)}, f32[2,2,384,128]{3,2,1,0:T(8,128)S(1)}, f32[2,2,128,128]{3,2,1,0...) custom-call(f32[2,2,128,384]{3,2,1,0:T(8,128)S(1)} %get-tuple-elemen, ...), custom_call_target="tpu_custom_call" | custom-call | tf_op jit(solution)/shard_map/exchange0/pallas_call | solution.py:419
  101.4 1.8 windows1.1
  103.3 54.5 %exchange1.1 = (f32[2,2,128,384]{3,2,1,0:T(8,128)S(1)}, f32[2,2,128,384]{3,2,1,0:T(8,128)S(1)}, f32[2,2,384,128]{3,2,1,0:T(8,128)S(1)}, f32[2,2,128,128]{3,2,1,0...) custom-call(f32[2,2,128,384]{3,2,1,0:T(8,128)S(1)} %get-tuple-elemen, ...), custom_call_target="tpu_custom_call" | custom-call | tf_op jit(solution)/shard_map/exchange1/pallas_call | solution.py:419
  157.8 6.6 %windows2.1 = (f32[2,2,512,256]{3,2,1,0:T(8,128)S(1)}, f32[2,2,128,384]{3,2,1,0:T(8,128)S(1)}, f32[2,2,384,128]{3,2,1,0:T(8,128)S(1)}, f32[2,2,128,128]{3,2,1,0:T(8,128)S(1)}) custom-call(s32[1,1]{1,0:T(1,128)S(6)} %copy.13.refs_0_, s32[1,1,4]{2,1,0:T(1,128)S(1)} %copy-done.8, s32[1,1,4]{2,1,0:T(1,128)S(1)} %copy-done.9, s32[1,1,4]{2,1,0:T(1,128)S(1)} %copy-done.10, ...), custom_call_target="tpu_custom_call" | custom-call | tf_op jit(solution)/shard_map/windows2/pallas_call | solution.py:395
  164.4 36.0 %exchange2.1 = (f32[2,2,128,384]{3,2,1,0:T(8,128)S(1)}, f32[2,2,384,128]{3,2,1,0:T(8,128)S(1)}, f32[2,2,128,128]{3,2,1,0:T(8,128)S(1)}) custom-call(f32[2,2,128,384]{3,2,1,0:T(8,128)S(1)} %get-tuple-element.69.refs_0_, f32[2,2,384,128]{3,2,1,0:T(8,128)S(1)} %get-tuple-element.70.refs_1_, f32[2,2,128,128]{3,2,1,0:T(8,128)S(1)} %get-tuple-element.71.refs_2_), custom_call_target="tpu_custom_call" | custom-call | tf_op jit(solution)/shard_map/exchange2/pallas_call | solution.py:419
  200.4 1.5 finish.1
  (18 shorter events, 0.1 us)
Async XLA Ops:
  2.1 29.2 %copy-start.11 = (f32[1,1,4,256,256]{4,3,2,1,0:T(8,128)S(1)}, f32[1,1,4,256,256]{4,3,2,1,0:T(8,128)}, u32[]{:S(2)}) copy-start(f32[1,1,4,256,256]{4,3,2,1,0:T(8,128)} %param.15) | copy-start | bytes 3145732
  2.1 29.2 %copy-start.12 = (bf16[768,256]{1,0:T(8,128)(2,1)S(1)}, bf16[768,256]{1,0:T(8,128)(2,1)}, u32[]{:S(2)}) copy-start(bf16[768,256]{1,0:T(8,128)(2,1)} %constant.23.clone.pick_t) | copy-start | bytes 1179652
  2.1 34.9 %collective-permute-start.2 = (f32[2,2,384,128]{3,2,1,0:T(8,128)}, f32[2,2,384,128]{3,2,1,0:T(8,128)S(1)}, u32[]{:S(2)}, u32[]{:S(2)}) collective-permute-start(f32[2,2,384,128]{3,2,1,0:T(8,128)} %slice.11), channel_id=1, source_target_pairs={{1,0},{2,1},{3,2},{4,3},{5,4},{6,5},{7,6},{9,8},{10,9},{11,10},{12... | collective-permute-start | bytes 2359304 | tf_op jit(solution)/shard_map/ppermute | solution.py:21
  7.2 22.0 %collective-permute-start.1 = (f32[2,2,128,128]{3,2,1,0:T(8,128)}, f32[2,2,128,128]{3,2,1,0:T(8,128)S(1)}, u32[]{:S(2)}, u32[]{:S(2)}) collective-permute-start(f32[2,2,128,128]{3,2,1,0:T(8,128)} %slice.10), channel_id=1, source_target_pairs={{1,0},{2,1},{3,2},{4,3},{5,4},{6,5},{7,6},{9,8},{10,9},{11,10},{12... | collective-permute-start | bytes 786440 | tf_op jit(solution)/shard_map/ppermute | solution.py:21
  11.5 24.6 %collective-permute-start = (f32[2,2,128,256]{3,2,1,0:T(8,128)}, f32[2,2,128,256]{3,2,1,0:T(8,128)S(1)}, u32[]{:S(2)}, u32[]{:S(2)}) collective-permute-start(f32[2,2,128,256]{3,2,1,0:T(8,128)} %slice.9), channel_id=1, source_target_pairs={{8,0},{16,8},{24,16},{9,1},{17,9},{25,17},{10,2},{18,10},{26,18},{... | collective-permute-start | bytes 1572872 | tf_op jit(solution)/shard_map/ppermute | solution.py:21
  12.8 24.2 %copy-start.3 = (f32[2,256,256]{2,1,0:T(8,128)S(1)}, f32[2,256,256]{2,1,0:T(8,128)}, u32[]{:S(2)}) copy-start(f32[2,256,256]{2,1,0:T(8,128)} %refs_14_.4) | copy-start | bytes 1572868
  29.2 6.9 %copy-start.6 = (f32[2,2,128,128]{3,2,1,0:T(8,128)}, f32[2,2,128,128]{3,2,1,0:T(8,128)S(1)}, u32[]{:S(2)}) copy-start(f32[2,2,128,128]{3,2,1,0:T(8,128)S(1)} %collective-permute-done.1.refs_7_) | copy-start | bytes 786436
  29.2 6.9 %collective-permute-start.3 = (f32[2,2,128,128]{3,2,1,0:T(8,128)S(1)}, f32[2,2,128,128]{3,2,1,0:T(8,128)S(1)}, u32[]{:S(2)}, u32[]{:S(2)}) collective-permute-start(f32[2,2,128,128]{3,2,1,0:T(8,128)S(1)} %collective-permute-done.1.refs_7_), channel_id=1, source_target_pairs={{8,0},{16,8},{24,16},{9,1},{17,9},{25,17},{10,2},{18,10},{26,18},{... | collective-permute-start | bytes 786440 | tf_op jit(solution)/shard_map/ppermute | solution.py:21
  31.2 5.7 %copy-start.2 = (f32[2,2,512,256]{3,2,1,0:T(8,128)S(1)}, f32[2,2,512,256]{3,2,1,0:T(8,128)}, u32[]{:S(2)}) copy-start(f32[2,2,512,256]{3,2,1,0:T(8,128)} %refs_5_.1) | copy-start | bytes 6291460
  31.3 1.1 copy-start.13
  32.5 4.5 %copy-start = (bf16[4,768,256]{2,1,0:T(8,128)(2,1)S(1)}, bf16[4,768,256]{2,1,0:T(8,128)(2,1)}, u32[]{:S(2)}) copy-start(bf16[4,768,256]{2,1,0:T(8,128)(2,1)} %constant.21.clone.refs_13_.refs_17_) | copy-start | bytes 4718596
  32.5 4.5 %copy-start.1 = (bf16[4,256,768]{2,1,0:T(8,128)(2,1)S(1)}, bf16[4,256,768]{2,1,0:T(8,128)(2,1)}, u32[]{:S(2)}) copy-start(bf16[4,256,768]{2,1,0:T(8,128)(2,1)} %constant.20.clone.refs_14_.refs_18_) | copy-start | bytes 4718596
  32.5 4.5 %copy-start.8 = (s32[1,1,4]{2,1,0:T(1,128)S(1)}, s32[1,1,4]{2,1,0:T(1,128)}, u32[]{:S(2)}) copy-start(s32[1,1,4]{2,1,0:T(1,128)} %refs_1_.5) | copy-start | bytes 52
  32.5 4.5 %copy-start.9 = (s32[1,1,4]{2,1,0:T(1,128)S(1)}, s32[1,1,4]{2,1,0:T(1,128)}, u32[]{:S(2)}) copy-start(s32[1,1,4]{2,1,0:T(1,128)} %refs_2_.5) | copy-start | bytes 52
  32.5 4.6 %copy-start.10 = (s32[1,1,4]{2,1,0:T(1,128)S(1)}, s32[1,1,4]{2,1,0:T(1,128)}, u32[]{:S(2)}) copy-start(s32[1,1,4]{2,1,0:T(1,128)} %refs_3_.5) | copy-start | bytes 52
  36.2 0.8 copy-start.4
  37.0 1.0 copy-start.5
  38.1 0.9 copy-start.7
